TPU v7x, 32 devices: a whole 2x2x4 slice. The times are simulated.
32 devices in a mesh: lat: 4 (over z), lon: 8 (over y, x, core).
Axes of the slice: x: 2, y: 2, z: 4, core: 2. Of those that a mesh axis runs over, the one named last changes fastest.
Arguments:
- control: float32 [4, 90, 32, 1024], P(None, None, 'lat', 'lon'), may hold values from -6 to 6
- kappa: float32 [4, 90, 32, 1024], P(None, None, 'lat', 'lon'), may hold values from 0.25 to 0.5
- pc_obs: bfloat16 [1024, 128, 300], P(('lat', 'lon')), may hold values from -6 to 6
- owner: int32 [1024, 1], P(('lat', 'lon')), may hold values from 0 to 31; in each aligned block of 32 rows (0 to 31, 32 to 63, ...) at most 2 rows name the same one
- columns: int32 [1024, 128], P(('lat', 'lon')), may hold values from 0 to 1023
- counts: int32 [1024], P(('lat', 'lon')), may hold values from 1 to 128, as said below
- jacobian: bfloat16 [360, 300], replicated, may hold values from -0.3125 to 0.3125
- obs_weight: float32 [300], replicated, may hold values from 0.3 to 3
Outputs:
- gradient: float32 [4, 90, 32, 1024], P(None, None, 'lat', 'lon')
Inputs may be any that keep to these rules, and one draw needn't show every extreme that they name: Among the 32 blocks of one device no owner is named more than 2 times, a bound that some block reaches. `counts`: the first block of every device is full.
All inputs are finite; a program needn't handle non-finite values.
Results may differ from a plain program's by a relative error of at most 0.0017.
Values may be sent and summed in bfloat16 or wider, within the bound.
A program may use at most 256 MiB of HBM per device.

v0:
```python
import jax
import jax.numpy as jnp
from jax import lax
from jax.experimental import pallas as pl
from jax.experimental.pallas import tpu as pltpu
from jax.sharding import PartitionSpec as P

CAP = 2
STEPS = 4
GROUP = 4


def ring(axis, step):
    count = lax.axis_size(axis)
    return [(i, (i + step) % count) for i in range(count)]


def rims(core, closed):
    north = lax.ppermute(core[:, -STEPS:].astype(jnp.bfloat16), "lat", ring("lat", 1)).astype(core.dtype)
    south = lax.ppermute(core[:, :STEPS].astype(jnp.bfloat16), "lat", ring("lat", -1)).astype(core.dtype)
    if closed:
        place = lax.axis_index("lat")
        zero = jnp.zeros((), core.dtype)
        north = jnp.where(place == 0, zero, north)
        south = jnp.where(place == lax.axis_size("lat") - 1, zero, south)
    main = jnp.concatenate([core, south, north], axis=1)
    planes = main.shape[0]
    head = main[:, :, :STEPS].reshape(planes, -1).astype(jnp.bfloat16)
    tail = main[:, :, -STEPS:].reshape(planes, -1).astype(jnp.bfloat16)
    west = lax.ppermute(tail, "lon", ring("lon", 1))
    east = lax.ppermute(head, "lon", ring("lon", -1))
    return main, jnp.concatenate([east, west], axis=1).astype(core.dtype)


def side_tile(side, rows, width):
    planes = side.shape[0]
    parts = side.reshape(planes, 2, rows, STEPS)
    gap = jnp.zeros((planes, rows, width - 2 * STEPS), side.dtype)
    return jnp.concatenate([parts[:, 0], gap, parts[:, 1]], axis=2)


def spread_kernel(field_ref, side_ref, coef_ref, coef_side_ref, *refs):
    out_ref = refs[-1]
    core, width = out_ref.shape[1:]
    rows, lanes = field_ref.shape[1], 2 * width

    @pl.loop(0, out_ref.shape[0], unroll=8)
    def _(i):
        coef = jnp.concatenate([coef_ref[i], coef_side_ref[i]], axis=1)
        field = jnp.concatenate([field_ref[i], side_ref[i]], axis=1)
        south = coef * pltpu.roll(coef, rows - 1, 0)
        east = coef * pltpu.roll(coef, lanes - 1, 1)
        for repeat in range(STEPS):
            down = south * (pltpu.roll(field, rows - 1, 0) - field)
            along = east * (pltpu.roll(field, lanes - 1, 1) - field)
            field = field + (down - pltpu.roll(down, 1, 0)) + (along - pltpu.roll(along, 1, 1))
        result = field[:core, :width]
        out_ref[i] = result + refs[0][i] if len(refs) > 1 else result


def spread(field, side, coef, coef_side, core, *base):
    planes, rows, width = field.shape
    batch = max(n for n in range(4, 41, 4) if planes % n == 0)
    wide = pl.BlockSpec((batch, rows, width), lambda i: (i, 0, 0))
    thin = pl.BlockSpec((batch, core, width), lambda i: (i, 0, 0))
    return pl.pallas_call(
        spread_kernel,
        out_shape=jax.ShapeDtypeStruct((planes, core, width), jnp.float32),
        grid=(planes // batch,),
        in_specs=[wide] * 4 + [thin] * len(base),
        out_specs=thin,
        cost_estimate=pl.CostEstimate(
            flops=planes * rows * width * 80, bytes_accessed=planes * rows * width * 20, transcendentals=0
        ),
    )(field, side, coef, coef_side, *base)


def pack_kernel(source_ref, *refs):
    blocks, (code_ref, out_ref, wide) = refs[:CAP], refs[CAP:]
    comps = blocks[0].shape[2]
    for k, block in enumerate(blocks):
        wide[0:comps, :] = jnp.transpose(block[0].astype(jnp.float32))
        code = code_ref[0, k : k + 1, :]
        low = jnp.bitwise_and(code, 31)
        wide[comps : comps + 1, :] = jnp.ones((1, wide.shape[1]), jnp.float32)
        wide[comps + 1 : comps + 2, :] = jnp.right_shift(code - low, 5).astype(jnp.float32)
        wide[comps + 2 : comps + 3, :] = low.astype(jnp.float32)
        wide[comps + 3 :, :] = jnp.zeros((wide.shape[0] - comps - 3, wide.shape[1]), jnp.float32)
        out_ref[k] = wide[...].astype(jnp.bfloat16)


def pack(pc_obs, source, code, height):
    blocks, soundings, comps = pc_obs.shape
    slots = code.shape[0]

    def place(k):
        return lambda i, src: (src[i * CAP + k], 0, 0)

    return pl.pallas_call(
        pack_kernel,
        out_shape=jax.ShapeDtypeStruct((slots, height, soundings), jnp.bfloat16),
        grid_spec=pltpu.PrefetchScalarGridSpec(
            num_scalar_prefetch=1,
            grid=(slots // CAP,),
            in_specs=[pl.BlockSpec((1, soundings, comps), place(k)) for k in range(CAP)]
            + [pl.BlockSpec((1, CAP, soundings), lambda i, src: (i, 0, 0))],
            out_specs=pl.BlockSpec((CAP, height, soundings), lambda i, src: (i, 0, 0)),
            scratch_shapes=[pltpu.VMEM((height, soundings), jnp.float32)],
        ),
    )(source, *([pc_obs] * CAP), code.reshape(slots // CAP, CAP, soundings))


def gather_kernel(comps, got_ref, sums_ref):
    height, cells = sums_ref.shape

    @pl.when(pl.program_id(0) == 0)
    def _():
        sums_ref[...] = jnp.zeros_like(sums_ref)

    base = height - 16
    lines = []
    for k in range(GROUP):
        tail = got_ref[k, base:height, :].astype(jnp.float32)
        high = tail[comps + 1 - base : comps + 2 - base, :]
        lines.append((high * 32.0 + tail[comps + 2 - base : comps + 3 - base, :]).astype(jnp.int32))
    code = jnp.concatenate(lines, axis=1)
    cell = lax.broadcasted_iota(jnp.int32, (cells, code.shape[1]), 0)
    hot = jnp.where(cell == code, 1.0, 0.0).astype(jnp.bfloat16)
    obs = jnp.concatenate([got_ref[k] for k in range(GROUP)], axis=1)
    sums_ref[...] += lax.dot_general(
        obs, hot, (((1,), (1,)), ((), ())), preferred_element_type=jnp.float32
    )


def column_sums(got, comps, cells):
    slots, height, soundings = got.shape
    return pl.pallas_call(
        lambda *refs: gather_kernel(comps, *refs),
        out_shape=jax.ShapeDtypeStruct((height, cells), jnp.float32),
        grid=(slots // GROUP,),
        in_specs=[pl.BlockSpec((GROUP, height, soundings), lambda i: (i, 0, 0))],
        out_specs=pl.BlockSpec((height, cells), lambda i: (0, 0)),
        compiler_params=pltpu.CompilerParams(vmem_limit_bytes=32 * 2**20),
    )(got)


def per_device(control, kappa, pc_obs, owner, columns, counts, jacobian, obs_weight):
    peers = lax.axis_size("lat") * lax.axis_size("lon")
    fields, levels, rows, width_dev = control.shape
    blocks, soundings, comps = pc_obs.shape
    cells = rows * width_dev
    height = -(-(comps + 3) // 16) * 16
    slots = peers * CAP
    target = owner[:, 0]
    index = jnp.arange(blocks, dtype=jnp.int32)
    same = (target[:, None] == target[None, :]) & (index[None, :] < index[:, None])
    position = target * CAP + jnp.sum(same.astype(jnp.int32), axis=1)
    hits = position[None, :] == jnp.arange(slots, dtype=jnp.int32)[:, None]
    source = jnp.sum(jnp.where(hits, index[None, :], 0), axis=1)
    order = jnp.arange(soundings, dtype=jnp.int32)
    code = jnp.where(order[None, :] < counts[:, None], columns, -32)
    code = -32 + jnp.sum(jnp.where(hits[:, :, None], code[None] + 32, 0), axis=1)
    sent = pack(pc_obs, source, code, height)
    planes = fields * levels
    extent = rows + 2 * STEPS
    start = control.reshape(planes, rows, width_dev)
    field, side = rims(start, False)
    coef, coef_side = rims(kappa.reshape(planes, rows, width_dev), True)
    sent, side, coef_side = lax.optimization_barrier((sent, side, coef_side))
    got = lax.all_to_all(sent, ("lat", "lon"), split_axis=0, concat_axis=0, tiled=True)
    coef_side = side_tile(coef_side, extent, width_dev)
    state = spread(field, side_tile(side, extent, width_dev), coef, coef_side, rows)
    table = state.astype(jnp.bfloat16).reshape(planes, cells)
    model = lax.dot_general(
        jacobian, table, (((0,), (0,)), ((), ())), preferred_element_type=jnp.float32
    )
    sums = column_sums(got, comps, cells)
    total = (sums[comps : comps + 1] * model - sums[:comps]) * obs_weight[:, None]
    total = total.astype(jnp.bfloat16).reshape(comps, rows, width_dev)
    total, total_side = rims(total, False)
    back, back_side = (
        lax.dot_general(
            jacobian, part.reshape(comps, -1), (((1,), (0,)), ((), ())), preferred_element_type=jnp.float32
        )
        for part in (total, total_side)
    )
    back = back.reshape(planes, extent, width_dev)
    result = spread(back, side_tile(back_side, extent, width_dev), coef, coef_side, rows, start)
    return result.reshape(control.shape)


def solution(mesh):
    placed = (
        P(None, None, "lat", "lon"),
        P(None, None, "lat", "lon"),
        P(("lat", "lon"), None, None),
        P(("lat", "lon"), None),
        P(("lat", "lon"), None),
        P(("lat", "lon")),
        P(),
        P(),
    )
    return jax.shard_map(
        per_device,
        mesh=mesh,
        in_specs=placed,
        out_specs=P(None, None, "lat", "lon"),
        check_vma=False,
    )
```

profile of v0, /device:TPU:1, one launch (start us, length us, event | category | flops | bytes accessed | tf_op | source)
XLA Modules:
  0.0 267.4 jit_solution(10859653367117298225)
XLA Ops:
  0.0 1.6 bitcast_convert_fusion.1
  1.6 1.1 fusion.18
  2.7 2.1 collective-permute-start.1
  4.8 2.0 collective-permute-start
  7.0 1.0 fusion.17
  8.0 3.3 %collective-permute-start.4 = (bf16[360,4,128]{2,1,0:T(4,128)(2,1)S(1)}, bf16[360,4,128]{2,1,0:T(4,128)(2,1)}, u32[]{:S(2)}, u32[]{:S(2)}) collective-permute-start(bf16[360,4,128]{2,1,0:T(4,128)(2,1)S(1)} %get-tuple-element.19), channel_id=1, source_target_pairs={{0,24},{8,0},{16,8},{24,16},{1,25},{9,1},{17,9},{25,17},{2,26},{10... | collective-permute-start | bytes 1105928 | tf_op jit(solution)/shard_map/ppermute | solution.py:20
  11.2 0.2 convert_reduce_fusion
  11.6 0.7 select_reduce_fusion.1.source_ref
  12.3 4.8 %copy.28.refs_0_.refs_1_ = bf16[32,128,300]{2,1,0:T(8,128)(2,1)} copy(bf16[32,128,300]{1,0,2:T(8,128)(2,1)} %param.10) | data formatting | bytes 4915200 | tf_op args[2]
  17.2 0.4 select_reduce_fusion
  17.5 0.6 broadcast_add_fusion
  18.1 20.2 %shard_map.82 = bf16[64,304,128]{2,1,0:T(8,128)(2,1)} custom-call(s32[64]{0:T(128)} %select_reduce_fusion.1.source_ref, bf16[32,128,300]{2,1,0:T(8,128)(2,1)} %copy.28.refs_0_.refs_1_, bf16[32,128,300]{2,1,0:T(8,128)(2,1)} %copy.28.refs_0_.refs_1_, s32[32,2,128]{2,1,0:T(2,128)} %bitcast.73), custom_call_target="tpu_custom_call" | custom-call | tf_op jit(solution)/shard_map/pallas_call | solution.py:99
  38.4 1.2 convert_element_type.49
  39.6 1.3 convert_element_type.48
  41.0 0.9 copy-done.4
  41.8 0.4 fusion.12
  42.3 2.3 fusion.15
  44.6 3.4 %copy.31 = bf16[360,16,4]{0,2,1:T(4,128)(2,1)} copy(bf16[360,16,4]{2,1,0:T(8,128)(2,1)} %get-tuple-element.16) | data formatting | bytes 92160 | tf_op jit(solution)/shard_map/slice | solution.py:29
  48.0 1.4 convert_element_type.51
  49.4 2.8 %collective-permute-start.3 = (bf16[360,64]{0,1:T(8,128)(2,1)}, bf16[360,64]{0,1:T(8,128)(2,1)}, u32[]{:S(2)}, u32[]{:S(2)}) collective-permute-start(bf16[360,64]{0,1:T(8,128)(2,1)} %convert_element_type.51), channel_id=1, source_target_pairs={{0,1},{1,2},{2,3},{3,4},{4,5},{5,6},{6,7},{7,0},{8,9},{9,10},{10,1... | collective-permute-start | bytes 138248 | tf_op jit(solution)/shard_map/ppermute | solution.py:30
  52.2 3.4 %copy.30 = bf16[360,16,4]{0,2,1:T(4,128)(2,1)} copy(bf16[360,16,4]{2,1,0:T(8,128)(2,1)} %get-tuple-element.15) | data formatting | bytes 92160 | tf_op jit(solution)/shard_map/slice | solution.py:28
  55.6 1.4 convert_element_type.50
  57.0 1.1 convert_select_fusion
  58.2 1.4 convert_select_fusion.1
  59.6 0.9 copy-done.7
  60.5 0.4 fusion.11
  61.0 2.3 fusion.14
  63.3 2.8 %copy.33 = bf16[360,16,4]{0,2,1:T(4,128)(2,1)S(1)} copy(bf16[360,16,4]{2,1,0:T(8,128)(2,1)} %get-tuple-element.14) | data formatting | bytes 92160 | tf_op jit(solution)/shard_map/slice | solution.py:29
  66.1 1.8 collective-permute-start.7
  67.9 2.8 %copy.32 = bf16[360,16,4]{0,2,1:T(4,128)(2,1)S(1)} copy(bf16[360,16,4]{2,1,0:T(8,128)(2,1)} %get-tuple-element.13) | data formatting | bytes 92160 | tf_op jit(solution)/shard_map/slice | solution.py:28
  70.8 0.8 maximum_convert_fusion
  71.7 2.6 collective-permute-done.6
  74.3 0.7 maximum_convert_fusion.1
  75.0 3.6 %all-to-all-start = ((bf16[64,304,128]{2,1,0:T(8,128)(2,1)}), bf16[64,304,128]{2,1,0:T(8,128)(2,1)}, u32[]{:S(2)}, u32[]{:S(2)}) async-start(bf16[64,304,128]{2,1,0:T(8,128)(2,1)} %shard_map.82), calls=%async_computation | async-start | bytes 9961472 | tf_op jit(solution)/shard_map/all_to_all | solution.py:170
  78.7 3.4 %pad_maximum_fusion.field_ref = f32[360,16,128]{2,1,0:T(8,128)} fusion(f32[360,4,128]{2,1,0:T(4,128)} %copy-done.3, f32[360,4,128]{2,1,0:T(4,128)} %copy-done.4, f32[360,8,128]{2,1,0:T(8,128)S(1)} %bitcast.59), kind=kLoop, calls=%fused_computation | loop fusion | flops 1474560 | bytes 5898240 | tf_op jit(solution)/shard_map/concatenate | solution.py:26
  82.2 2.1 pad_maximum_fusion.1.coef_ref
  84.3 0.7 fusion.20
  85.0 2.6 copy.48
  87.6 3.1 %copy.47 = f32[360,1,16,4]{3,2,0,1:T(8,128)} copy(f32[360,1,16,4]{0,3,2,1:T(4,128)S(1)} %get-tuple-element.25) | data formatting | bytes 184320
  90.6 0.7 reshape.82
  91.4 1.0 fusion.21
  92.3 3.2 %copy.46 = f32[360,1,16,4]{3,2,0,1:T(8,128)} copy(f32[360,1,16,4]{0,3,2,1:T(4,128)S(1)} %get-tuple-element.28) | data formatting | bytes 184320
  95.5 3.2 %copy.45 = f32[360,1,16,4]{3,2,0,1:T(8,128)} copy(f32[360,1,16,4]{0,3,2,1:T(4,128)S(1)} %get-tuple-element.27) | data formatting | bytes 184320
  98.7 8.0 %pad_maximum_fusion.3 = (f32[360,16,128]{2,1,0:T(8,128)}, f32[360,16,128]{2,1,0:T(8,128)}) fusion(f32[360,16,4]{2,1,0:T(8,128)S(1)} %bitcast.62, f32[360,16,4]{2,1,0:T(8,128)} %bitcast.63, f32[128]{0:T(128)S(1)} %pad.12.clone, f32[360,16,4]{2,1,0:T(8,128)} %bitcast.64, f32[360,16,4]{2,1,0:T(8,128)} %bitcast.65), kind=kLoop, calls=%fused_computation.3 | loop fusion | flops 2949120 | bytes 6267392 | tf_op jit(solution)/shard_map/concatenate | solution.py:39
  106.7 29.1 %shard_map.84 = f32[360,8,128]{2,1,0:T(8,128)} custom-call(f32[360,16,128]{2,1,0:T(8,128)} %pad_maximum_fusion.field_ref, f32[360,16,128]{2,1,0:T(8,128)} %get-tuple-element.30.side_ref, f32[360,16,128]{2,1,0:T(8,128)} %pad_maximum_fusion.1.coef_ref, f32[360,16,128]{2,1,0:T(8,128)} %get-tuple-element.29.coef_side_ref), custom_call_target="tpu_custom_call" | custom-call | flops 58982400 | bytes 14745600 | tf_op jit(solution)/shard_map/pallas_call | solution.py:66
  135.8 1.4 convert_element_type.58
  137.2 52.2 %all-to-all-done.refs_0_ = bf16[64,304,128]{2,1,0:T(8,128)(2,1)} async-done(((bf16[64,304,128]{2,1,0:T(8,128)(2,1)}), bf16[64,304,128]{2,1,0:T(8,128)(2,1)}, u32[]{:S(2)}, u32[]{:S(2)}) %all-to-all-start) | async-done | bytes 4980768 | tf_op jit(solution)/shard_map/all_to_all | solution.py:170
  189.5 13.2 %shard_map.83 = f32[304,1024]{1,0:T(8,128)S(1)} custom-call(bf16[64,304,128]{2,1,0:T(8,128)(2,1)} %all-to-all-done.refs_0_), custom_call_target="tpu_custom_call" | custom-call | tf_op jit(solution)/shard_map/pallas_call | solution.py:137
  202.7 0.5 fusion.3
  203.2 0.4 copy.44
  203.7 3.3 %collective-permute-start.8 = (bf16[300,4,128]{0,2,1:T(8,128)(2,1)S(1)}, bf16[300,4,128]{0,2,1:T(8,128)(2,1)S(1)}, u32[]{:S(2)}, u32[]{:S(2)}) collective-permute-start(bf16[300,4,128]{0,2,1:T(8,128)(2,1)S(1)} %get-tuple-element.17), channel_id=1, source_target_pairs={{0,24},{8,0},{16,8},{24,16},{1,25},{9,1},{17,9},{25,17},{2,26},{10... | collective-permute-start | bytes 921608 | tf_op jit(solution)/shard_map/ppermute | solution.py:20
  206.9 8.3 %collective-permute-done.9 = bf16[300,4,128]{0,2,1:T(8,128)(2,1)S(1)} collective-permute-done((bf16[300,4,128]{0,2,1:T(8,128)(2,1)S(1)}, bf16[300,4,128]{0,2,1:T(8,128)(2,1)S(1)}, u32[]{:S(2)}, u32[]{:S(2)}) %collective-permute-start.9) | collective-permute-done | bytes 307232 | tf_op jit(solution)/shard_map/ppermute | solution.py:19
  215.3 6.6 %collective-permute-done.8 = bf16[300,4,128]{0,2,1:T(8,128)(2,1)S(1)} collective-permute-done((bf16[300,4,128]{0,2,1:T(8,128)(2,1)S(1)}, bf16[300,4,128]{0,2,1:T(8,128)(2,1)S(1)}, u32[]{:S(2)}, u32[]{:S(2)}) %collective-permute-start.8) | collective-permute-done | bytes 307232 | tf_op jit(solution)/shard_map/ppermute | solution.py:20
  221.9 0.3 pad_maximum_fusion.5
  222.3 2.3 collective-permute-start.11
  224.6 0.3 collective-permute-start.10
  224.9 1.0 convolution_bitcast_fusion
  225.9 2.2 copy.52
  228.1 0.3 collective-permute-done.10
  228.4 0.3 convolution_bitcast_fusion.1
  228.9 1.7 copy.50
  230.7 3.1 %copy.49 = f32[360,1,16,4]{3,2,0,1:T(8,128)} copy(f32[360,1,16,4]{0,3,2,1:T(4,128)S(1)} %get-tuple-element.23) | data formatting | bytes 184320
  233.8 4.4 %pad_maximum_fusion.4.side_ref = f32[360,16,128]{2,1,0:T(8,128)} fusion(f32[360,16,4]{2,1,0:T(8,128)S(1)} %bitcast.67, f32[360,16,4]{2,1,0:T(8,128)} %bitcast.68, f32[128]{0:T(128)S(1)} %pad.12.clone), kind=kLoop, calls=%fused_computation.4 | loop fusion | flops 1474560 | bytes 3133952 | tf_op jit(solution)/shard_map/concatenate | solution.py:39
  238.2 29.2 %shard_map.85 = f32[360,8,128]{2,1,0:T(8,128)} custom-call(f32[360,16,128]{2,1,0:T(8,128)} %bitcast.66, f32[360,16,128]{2,1,0:T(8,128)} %pad_maximum_fusion.4.side_ref, f32[360,16,128]{2,1,0:T(8,128)} %pad_maximum_fusion.1.coef_ref, f32[360,16,128]{2,1,0:T(8,128)} %get-tuple-element.29.coef_side_ref, f32[360,8,128]{2,1,0:T(8,128)} %bitcast.57), custom_call_target="tpu_custom_call" | custom-call | flops 58982400 | bytes 14745600 | tf_op jit(solution)/shard_map/pallas_call | solution.py:66
  (56 shorter events, 1.1 us)
Async XLA Ops:
  0.0 202.6 %copy-start = (bf16[360,300]{0,1:T(8,128)(2,1)S(1)}, bf16[360,300]{0,1:T(8,128)(2,1)}, u32[]{:S(2)}) copy-start(bf16[360,300]{0,1:T(8,128)(2,1)} %param.14) | copy-start | bytes 648004
  0.0 6.9 %copy-start.2 = (f32[4,90,8,128]{3,2,1,0:T(8,128)S(1)}, f32[4,90,8,128]{3,2,1,0:T(8,128)}, u32[]{:S(2)}) copy-start(f32[4,90,8,128]{3,2,1,0:T(8,128)} %param.9) | copy-start | bytes 4423684
  1.6 9.7 %copy-start.13 = (s32[32,1]{0,1:T(1,128)S(1)}, s32[32,1]{0,1:T(1,128)}, u32[]{:S(2)}) copy-start(s32[32,1]{0,1:T(1,128)} %param.11) | copy-start | bytes 388
  1.6 9.9 %copy-start.10 = (s32[32,128]{1,0:T(8,128)S(1)}, s32[32,128]{1,0:T(8,128)}, u32[]{:S(2)}) copy-start(s32[32,128]{1,0:T(8,128)} %param.12) | copy-start | bytes 49156
  1.6 9.9 %copy-start.11 = (s32[32]{0:T(128)S(1)}, s32[32]{0:T(128)}, u32[]{:S(2)}) copy-start(s32[32]{0:T(128)} %param.13) | copy-start | bytes 388
  2.7 35.7 %collective-permute-start.1 = (bf16[360,4,128]{2,1,0:T(4,128)(2,1)}, bf16[360,4,128]{2,1,0:T(4,128)(2,1)}, u32[]{:S(2)}, u32[]{:S(2)}) collective-permute-start(bf16[360,4,128]{2,1,0:T(4,128)(2,1)} %get-tuple-element.22), channel_id=1, source_target_pairs={{0,8},{8,16},{16,24},{24,0},{1,9},{9,17},{17,25},{25,1},{2,10},{10... | collective-permute-start | bytes 1105928 | tf_op jit(solution)/shard_map/ppermute | solution.py:19
  4.8 34.7 %collective-permute-start = (bf16[360,4,128]{2,1,0:T(4,128)(2,1)}, bf16[360,4,128]{2,1,0:T(4,128)(2,1)}, u32[]{:S(2)}, u32[]{:S(2)}) collective-permute-start(bf16[360,4,128]{2,1,0:T(4,128)(2,1)} %get-tuple-element.21), channel_id=1, source_target_pairs={{0,24},{8,0},{16,8},{24,16},{1,25},{9,1},{17,9},{25,17},{2,26},{10... | collective-permute-start | bytes 1105928 | tf_op jit(solution)/shard_map/ppermute | solution.py:20
  8.0 49.1 %collective-permute-start.5 = (bf16[360,4,128]{2,1,0:T(4,128)(2,1)}, bf16[360,4,128]{2,1,0:T(4,128)(2,1)}, u32[]{:S(2)}, u32[]{:S(2)}) collective-permute-start(bf16[360,4,128]{2,1,0:T(4,128)(2,1)} %get-tuple-element.20), channel_id=1, source_target_pairs={{0,8},{8,16},{16,24},{24,0},{1,9},{9,17},{17,25},{25,1},{2,10},{10... | collective-permute-start | bytes 1105928 | tf_op jit(solution)/shard_map/ppermute | solution.py:19
  8.0 50.2 %collective-permute-start.4 = (bf16[360,4,128]{2,1,0:T(4,128)(2,1)S(1)}, bf16[360,4,128]{2,1,0:T(4,128)(2,1)}, u32[]{:S(2)}, u32[]{:S(2)}) collective-permute-start(bf16[360,4,128]{2,1,0:T(4,128)(2,1)S(1)} %get-tuple-element.19), channel_id=1, source_target_pairs={{0,24},{8,0},{16,8},{24,16},{1,25},{9,1},{17,9},{25,17},{2,26},{10... | collective-permute-start | bytes 1105928 | tf_op jit(solution)/shard_map/ppermute | solution.py:20
  38.4 3.4 %copy-start.1 = (f32[4,90,8,128]{3,2,1,0:T(8,128)S(1)}, f32[4,90,8,128]{3,2,1,0:T(8,128)}, u32[]{:S(2)}) copy-start(f32[4,90,8,128]{3,2,1,0:T(8,128)} %param.8) | copy-start | bytes 4423684
  39.6 1.4 copy-start.3
  40.9 0.9 copy-start.4
  49.4 21.4 %collective-permute-start.3 = (bf16[360,64]{0,1:T(8,128)(2,1)}, bf16[360,64]{0,1:T(8,128)(2,1)}, u32[]{:S(2)}, u32[]{:S(2)}) collective-permute-start(bf16[360,64]{0,1:T(8,128)(2,1)} %convert_element_type.51), channel_id=1, source_target_pairs={{0,1},{1,2},{2,3},{3,4},{4,5},{5,6},{6,7},{7,0},{8,9},{9,10},{10,1... | collective-permute-start | bytes 138248 | tf_op jit(solution)/shard_map/ppermute | solution.py:30
  57.0 13.8 %collective-permute-start.2 = (bf16[360,64]{0,1:T(8,128)(2,1)}, bf16[360,64]{0,1:T(8,128)(2,1)}, u32[]{:S(2)}, u32[]{:S(2)}) collective-permute-start(bf16[360,64]{0,1:T(8,128)(2,1)} %convert_element_type.50), channel_id=1, source_target_pairs={{0,7},{1,0},{2,1},{3,2},{4,3},{5,4},{6,5},{7,6},{8,15},{9,8},{10,9... | collective-permute-start | bytes 138248 | tf_op jit(solution)/shard_map/ppermute | solution.py:31
  58.2 1.4 copy-start.5
  59.6 0.9 copy-start.7
  66.1 5.6 %collective-permute-start.7 = (bf16[360,64]{0,1:T(8,128)(2,1)S(1)}, bf16[360,64]{0,1:T(8,128)(2,1)S(1)}, u32[]{:S(2)}, u32[]{:S(2)}) collective-permute-start(bf16[360,64]{0,1:T(8,128)(2,1)S(1)} %convert_element_type.56), channel_id=1, source_target_pairs={{0,1},{1,2},{2,3},{3,4},{4,5},{5,6},{6,7},{7,0},{8,9},{9,10},{10,1... | collective-permute-start | bytes 138248 | tf_op jit(solution)/shard_map/ppermute | solution.py:30
  70.8 3.6 %collective-permute-start.6 = (bf16[360,64]{0,1:T(8,128)(2,1)S(1)}, bf16[360,64]{0,1:T(8,128)(2,1)S(1)}, u32[]{:S(2)}, u32[]{:S(2)}) collective-permute-start(bf16[360,64]{0,1:T(8,128)(2,1)S(1)} %convert_element_type.55), channel_id=1, source_target_pairs={{0,7},{1,0},{2,1},{3,2},{4,3},{5,4},{6,5},{7,6},{8,15},{9,8},{10,9... | collective-permute-start | bytes 138248 | tf_op jit(solution)/shard_map/ppermute | solution.py:31
  75.0 114.4 %all-to-all-start = ((bf16[64,304,128]{2,1,0:T(8,128)(2,1)}), bf16[64,304,128]{2,1,0:T(8,128)(2,1)}, u32[]{:S(2)}, u32[]{:S(2)}) async-start(bf16[64,304,128]{2,1,0:T(8,128)(2,1)} %shard_map.82), calls=%async_computation | async-start | bytes 9961472 | tf_op jit(solution)/shard_map/all_to_all | solution.py:170
  78.7 3.4 %copy-start.6 = (f32[360,4,128]{2,1,0:T(4,128)S(1)}, f32[360,4,128]{2,1,0:T(4,128)}, u32[]{:S(2)}) copy-start(f32[360,4,128]{2,1,0:T(4,128)} %copy-done.5) | copy-start | bytes 2211844
  78.7 3.4 %copy-start.8 = (f32[360,4,128]{2,1,0:T(4,128)S(1)}, f32[360,4,128]{2,1,0:T(4,128)}, u32[]{:S(2)}) copy-start(f32[360,4,128]{2,1,0:T(4,128)} %copy-done.7) | copy-start | bytes 2211844
  82.2 2.1 copy-start.9
  137.2 65.4 %copy-start.12 = (f32[300]{0:T(512)S(1)}, f32[300]{0:T(512)}, u32[]{:S(2)}) copy-start(f32[300]{0:T(512)} %param.15) | copy-start | bytes 3604
  203.6 11.7 %collective-permute-start.9 = (bf16[300,4,128]{0,2,1:T(8,128)(2,1)S(1)}, bf16[300,4,128]{0,2,1:T(8,128)(2,1)S(1)}, u32[]{:S(2)}, u32[]{:S(2)}) collective-permute-start(bf16[300,4,128]{0,2,1:T(8,128)(2,1)S(1)} %get-tuple-element.18), channel_id=1, source_target_pairs={{0,8},{8,16},{16,24},{24,0},{1,9},{9,17},{17,25},{25,1},{2,10},{10... | collective-permute-start | bytes 921608 | tf_op jit(solution)/shard_map/ppermute | solution.py:19
  203.7 18.2 %collective-permute-start.8 = (bf16[300,4,128]{0,2,1:T(8,128)(2,1)S(1)}, bf16[300,4,128]{0,2,1:T(8,128)(2,1)S(1)}, u32[]{:S(2)}, u32[]{:S(2)}) collective-permute-start(bf16[300,4,128]{0,2,1:T(8,128)(2,1)S(1)} %get-tuple-element.17), channel_id=1, source_target_pairs={{0,24},{8,0},{16,8},{24,16},{1,25},{9,1},{17,9},{25,17},{2,26},{10... | collective-permute-start | bytes 921608 | tf_op jit(solution)/shard_map/ppermute | solution.py:20
  222.3 5.8 %collective-permute-start.11 = (bf16[300,64]{0,1:T(8,128)(2,1)S(1)}, bf16[300,64]{0,1:T(8,128)(2,1)S(1)}, u32[]{:S(2)}, u32[]{:S(2)}) collective-permute-start(bf16[300,64]{0,1:T(8,128)(2,1)S(1)} %reshape.89), channel_id=1, source_target_pairs={{0,1},{1,2},{2,3},{3,4},{4,5},{5,6},{6,7},{7,0},{8,9},{9,10},{10,1... | collective-permute-start | bytes 115208 | tf_op jit(solution)/shard_map/ppermute | solution.py:30
  224.6 3.8 %collective-permute-start.10 = (bf16[300,64]{0,1:T(8,128)(2,1)S(1)}, bf16[300,64]{0,1:T(8,128)(2,1)S(1)}, u32[]{:S(2)}, u32[]{:S(2)}) collective-permute-start(bf16[300,64]{0,1:T(8,128)(2,1)S(1)} %reshape.88), channel_id=1, source_target_pairs={{0,7},{1,0},{2,1},{3,2},{4,3},{5,4},{6,5},{7,6},{8,15},{9,8},{10,9... | collective-permute-start | bytes 115208 | tf_op jit(solution)/shard_map/ppermute | solution.py:31
where the time goes:
time: 271 us; the launch traced here: 267 us
  Pallas kernels  91.7 us (34%)
  waiting for transfers between devices  70.2 us (26%)
  local copies, waits for them, and re-layouts  51 us (19%)
  other arithmetic  30.8 us (11%)
  starting transfers between devices  21.5 us (8%)
    pallas_call x2, Pallas kernels, spread(): pl.pallas_call(spread_kernel, out_shape=jax.ShapeDtypeStruct((planes, cor...  58.3 us
    all_to_all x1, waiting for transfers between devices, per_device(): lax.all_to_all(sent, ('lat', 'lon'), split_axis=0, concat_axis=0, tiled=T...  52.2 us
    unnamed x36, local copies, waits for them, and re-layouts  25.5 us
    pallas_call x1, Pallas kernels, pack(): pl.pallas_call(pack_kernel, out_shape=jax.ShapeDtypeStruct((slots, height...  20.2 us
    pallas_call x1, Pallas kernels, column_sums(): pl.pallas_call(lambda *refs: gather_kernel(comps, *refs), out_shape=jax.S...  13.2 us
    concatenate x2, other arithmetic, side_tile(): return jnp.concatenate([parts[:, 0], gap, parts[:, 1]], axis=2)  12.4 us
    slice x5, local copies, waits for them, and re-layouts, rims(): head = main[:, :, :STEPS].reshape(planes, -1).astype(jnp.bfloat16)  10.9 us
    ppermute x3, starting transfers between devices, rims(): lax.ppermute(core[:, :STEPS].astype(jnp.bfloat16), 'lat', ring('lat', -1))  8.54 us
  transfers between devices with their start and end apart: 13, of which 5 were waited for; matrix products, arithmetic and copies ran while one was open for 25% of the time, Pallas kernels for 18%

commit v1 on v0

v1 whole, which is shorter than its diff:
```python
import functools

import jax
import jax.numpy as jnp
from jax import lax
from jax.experimental import pallas as pl
from jax.experimental.pallas import tpu as pltpu
from jax.sharding import PartitionSpec as P

CAP = 2
STEPS = 4
LANES = 128
EDGE = 8
HEAD = 4
COUNT_BASE = 64
MESH = pl.DeviceIdType.MESH
F32 = jnp.float32
BF16 = jnp.bfloat16
SIDES = ((0, -1), (0, 1), (-1, -1), (-1, 1), (1, -1), (1, 1))


def iota(shape, dim):
    return lax.broadcasted_iota(jnp.int32, shape, dim)


def pack_kernel(group, owner_ref, obs_ref, columns_ref, counts_ref, out_ref, wide, source):
    blocks = columns_ref.shape[0]
    comps = obs_ref.shape[0]
    height = out_ref.shape[1]
    slots = source.shape[0]

    @pl.when(pl.program_id(0) == 0)
    def _():
        @pl.loop(0, slots)
        def _(t):
            source[t] = -1

        @pl.loop(0, blocks)
        def _(b):
            first = owner_ref[b] * CAP
            source[jnp.where(source[first] < 0, first, first + 1)] = b

        columns = columns_ref[...]
        valid = iota(columns.shape, 1) < counts_ref[...]
        low = jnp.bitwise_and(columns, 31)
        high = jnp.where(valid, jnp.right_shift(columns - low, 5), -1)
        wide[0:blocks, :] = jnp.ones(columns.shape, F32)
        wide[blocks : 2 * blocks, :] = high.astype(F32)
        wide[2 * blocks : 3 * blocks, :] = low.astype(F32)
        wide[3 * blocks : 4 * blocks, :] = jnp.zeros(columns.shape, F32)

        @pl.loop(0, comps, unroll=4)
        def _(c):
            start = pl.multiple_of((HEAD + c) * blocks, blocks)
            wide[pl.ds(start, blocks), :] = obs_ref[c].astype(F32)

        rest = (HEAD + comps) * blocks
        if rest < wide.shape[0]:
            wide[rest:, :] = jnp.zeros((wide.shape[0] - rest, wide.shape[1]), F32)

    for g in range(group):
        block = source[pl.program_id(0) * group + g]
        rows = wide[pl.ds(jnp.maximum(block, 0), height, stride=blocks), :]
        out_ref[g] = jnp.where(block < 0, -1.0, rows).astype(BF16)


def pack(pc_obs, owner, columns, counts, peers, height):
    blocks, soundings, comps = pc_obs.shape
    slots = peers * CAP
    group = 8
    return pl.pallas_call(
        functools.partial(pack_kernel, group),
        out_shape=jax.ShapeDtypeStruct((slots, height, soundings), BF16),
        grid_spec=pltpu.PrefetchScalarGridSpec(
            num_scalar_prefetch=1,
            grid=(slots // group,),
            in_specs=[
                pl.BlockSpec((comps, blocks, soundings), lambda i, s: (0, 0, 0)),
                pl.BlockSpec((blocks, soundings), lambda i, s: (0, 0)),
                pl.BlockSpec((blocks, 1), lambda i, s: (0, 0)),
            ],
            out_specs=pl.BlockSpec((group, height, soundings), lambda i, s: (i, 0, 0)),
            scratch_shapes=[
                pltpu.VMEM((height * blocks, soundings), F32),
                pltpu.SMEM((slots,), jnp.int32),
            ],
        ),
        compiler_params=pltpu.CompilerParams(vmem_limit_bytes=56 * 2**20),
    )(owner[:, 0], jnp.transpose(pc_obs, (2, 0, 1)), columns, counts[:, None])


def main_kernel(
    n_lat, n_lon, planes, parts, order,
    sent, control, kappa, jac, weight, out,
    recv, part_out, part_in, sums, number, model,
    field, coef, south, east, raw, band_out, band_in, tile_f, tile_out, tile_in,
    total, total_north, total_south, side_out, side_in,
    load_sem, own_sem, blk_send, blk_recv, part_send, part_recv,
    band_send, band_recv, tile_send, tile_recv, row_send, row_recv, side_send, side_recv, store_sem,
):
    lat, lon = lax.axis_index("lat"), lax.axis_index("lon")
    height, cells = sums.shape
    chunks, extent, wide, _ = field.shape
    rows = extent - 2 * STEPS
    width = wide - 2 * EDGE
    area = planes * rows
    step_rows = LANES * rows

    def remote(src, dst, send, recv_, to):
        return pltpu.make_async_remote_copy(
            src_ref=src, dst_ref=dst, send_sem=send, recv_sem=recv_, device_id=to, device_id_type=MESH
        )

    def block_copy(d, h, i):
        lo, size = parts[h]
        return remote(
            sent.at[lax.rem(lat + order[d], n_lat), lax.rem(lon + i, n_lon), :, pl.ds(lo, size), :],
            recv.at[d, i, :, pl.ds(lo, size), :],
            blk_send.at[d, h, i], blk_recv.at[d, h, i], (lat, lax.rem(lon + i, n_lon)),
        )

    def own_copy(d):
        return pltpu.make_async_copy(
            sent.at[lax.rem(lat + order[d], n_lat), lon], recv.at[d, 0], own_sem.at[d]
        )

    def part_copy(d, h):
        lo, size = parts[h]
        return remote(
            part_out.at[d, pl.ds(lo, size), :], part_in.at[d, pl.ds(lo, size), :],
            part_send.at[d, h], part_recv.at[d, h], (lax.rem(lat + order[d], n_lat), lon),
        )

    def band_copy(a, s):
        return remote(
            band_out.at[a, pl.ds((1 - s) * (rows - STEPS), STEPS)], band_in.at[a, s],
            band_send.at[a, s], band_recv.at[a, s], (lat + (1 - 2 * s), lon),
        )

    def peer(k):
        return (lat - SIDES[k][0], lax.rem(lon - SIDES[k][1] + n_lon, n_lon))

    def tile_copy(a, k):
        return remote(tile_out.at[a], tile_in.at[a, k], tile_send.at[a, k], tile_recv.at[a, k], peer(k))

    def row_copy(h, s):
        lo, size = parts[h]
        span = STEPS * width
        return remote(
            total.at[pl.ds(lo, size), pl.ds((1 - s) * (rows * width - span), span)],
            (total_north if s == 0 else total_south).at[pl.ds(lo, size), :],
            row_send.at[h, s], row_recv.at[h, s], (lat + (1 - 2 * s), lon),
        )

    def side_copy(h, k):
        lo, size = parts[h]
        return remote(
            side_out.at[pl.ds(lo, size), :], side_in.at[k, pl.ds(lo, size), :],
            side_send.at[h, k], side_recv.at[h, k], peer(k),
        )

    def has(step):
        return (lat + step >= 0) & (lat + step < n_lat)

    def only(step, act):
        if step == 0:
            act()
        else:
            pl.when(has(step))(act)

    for d in range(n_lat):
        for h in range(len(parts)):
            @pl.loop(1, n_lon)
            def _(i):
                block_copy(d, h, i).start()
        own_copy(d).start()

    loads = [
        pltpu.make_async_copy(ref, raw.at[a, pl.ds(0, area), :], load_sem.at[a])
        for a, ref in enumerate((control, kappa))
    ]
    for load in loads:
        load.start()
    sub = iota((EDGE, LANES), 0)

    for a, grid in enumerate((field, coef)):
        loads[a].wait()
        if chunks * step_rows > area:
            raw[a, area:, :] = jnp.zeros((chunks * step_rows - area, width), F32)

        @pl.loop(0, rows)
        def _(r):
            for j in range(chunks):
                turned = jnp.transpose(raw[a, pl.ds(j * step_rows + r, LANES, stride=rows), :])
                grid[j, STEPS + r, EDGE : EDGE + width, :] = turned
                band_out[a, r, j] = turned.astype(BF16)
                tile_f[j, r] = jnp.where(sub < STEPS, turned[:EDGE], turned[width - EDGE :])

        tile_out[a] = tile_f[...].reshape(chunks, rows * EDGE, LANES).astype(BF16)
        for s in range(2):
            only(1 - 2 * s, lambda: band_copy(a, s).start())
        for k in range(len(SIDES)):
            only(-SIDES[k][0], lambda: tile_copy(a, k).start())

    def reduce(d, h):
        lo, size = parts[h]

        @pl.loop(1, n_lon)
        def _(i):
            block_copy(d, h, i).wait_recv()

        if h == 0:
            own_copy(d).wait()
        heads = [recv[d, i, k, 0:16, :].astype(F32) for i in range(n_lon) for k in range(CAP)]
        code = jnp.concatenate([x[1:2] * 32.0 + x[2:3] for x in heads], axis=1).astype(jnp.int32)
        tile = 256
        line = iota((size, tile), 0)

        @pl.loop(0, cells // tile)
        def _(n):
            obs = jnp.concatenate(
                [recv[d, i, k, lo : lo + size, :] for i in range(n_lon) for k in range(CAP)], axis=1
            )
            hot = jnp.where(iota((tile, code.shape[1]), 0) == code - n * tile, 1.0, 0.0).astype(BF16)
            part = lax.dot_general(obs, hot, (((1,), (1,)), ((), ())), preferred_element_type=F32)
            at = pl.ds(pl.multiple_of(n * tile, tile), tile)
            if order[d] == 0:
                sums[lo : lo + size, at] = part
            else:
                if h == 0:
                    count = part[0:1]
                    high = jnp.floor(count * (1.0 / COUNT_BASE))
                    part = jnp.where(line == 0, count - high * COUNT_BASE, jnp.where(line == 1, high, part))
                part_out[d, lo : lo + size, at] = part.astype(BF16)

        if order[d] != 0:
            part_copy(d, h).start()

    def fill_edges(a, grid):
        def band(s):
            first = (rows + STEPS) * s

            def arrived():
                band_copy(a, s).wait_recv()
                for r in range(STEPS):
                    for j in range(chunks):
                        grid[j, first + r, EDGE : EDGE + width, :] = band_in[a, s, r, j].astype(F32)

            def closed():
                for r in range(STEPS):
                    for j in range(chunks):
                        grid[j, first + r] = jnp.zeros((wide, LANES), F32)

            pl.when(has(2 * s - 1))(arrived)
            pl.when(jnp.logical_not(has(2 * s - 1)))(closed)

        for s in range(2):
            band(s)

        def sides(west, count, place, source_row):
            tile_copy(a, west).wait_recv()
            tile_copy(a, west + 1).wait_recv()
            shape = (chunks, rows, EDGE, LANES)
            both = [tile_in[a, k].astype(F32).reshape(shape) for k in (west, west + 1)]
            for j in range(chunks):
                for r in range(count):
                    tile = jnp.where(sub < STEPS, both[1][j, source_row + r], both[0][j, source_row + r])
                    grid[j, place + r, 0:EDGE, :] = tile
                    grid[j, place + r, EDGE + width :, :] = tile

        sides(0, rows, STEPS, 0)
        only(-1, lambda: sides(2, STEPS, 0, rows - STEPS))
        only(1, lambda: sides(4, STEPS, rows + STEPS, 0))

    def spread():
        for step in range(STEPS):
            first, last = step + 1, extent - 1 - step

            @pl.loop(0, chunks)
            def _(j):
                here = field[j, first]
                above = south[j, first - 1] * (here - field[j, first - 1])

                def line(r, carry):
                    here, above = carry
                    below = field[j, r + 1]
                    down = south[j, r] * (below - here)
                    along = east[j, r] * (pltpu.roll(here, wide - 1, 0) - here)
                    field[j, r] = here + (down - above) + (along - pltpu.roll(along, 1, 0))
                    return below, down

                lax.fori_loop(first, last, line, (here, above))

    reduce(0, 0)
    for h in range(1, len(parts)):
        reduce(0, h)

    fill_edges(1, coef)

    @pl.loop(0, chunks)
    def _(j):
        @pl.loop(0, extent - 1)
        def _(r):
            here = coef[j, r]
            south[j, r] = here * coef[j, r + 1]
            east[j, r] = here * pltpu.roll(here, wide - 1, 0)

    fill_edges(0, field)
    spread()

    @pl.loop(0, rows)
    def _(r):
        state = jnp.concatenate(
            [field[j, STEPS + r, EDGE : EDGE + width, :].astype(BF16) for j in range(chunks)], axis=1
        )
        model[:, pl.ds(pl.multiple_of(r * width, width), width)] = lax.dot_general(
            jac[...], state, (((1,), (1,)), ((), ())), preferred_element_type=F32
        )

    for d in range(1, n_lat):
        for h in range(len(parts)):
            reduce(d, h)

    for s, ref in enumerate((total_north, total_south)):
        def blank():
            ref[...] = jnp.zeros(ref.shape, BF16)
            side_in[2 + 2 * s] = jnp.zeros(side_in.shape[1:], BF16)
            side_in[3 + 2 * s] = jnp.zeros(side_in.shape[1:], BF16)

        pl.when(jnp.logical_not(has(2 * s - 1)))(blank)

    away = [d for d in range(n_lat) if order[d] != 0]
    for h, (lo, size) in enumerate(parts):
        for d in away:
            part_copy(d, h).wait_recv()
        if h == 0:
            count = sums[0:8, :][0:1]
            for d in away:
                digits = part_in[d, 0:16, :].astype(F32)
                count = count + digits[0:1] + digits[1:2] * COUNT_BASE
            number[...] = jnp.broadcast_to(count, number.shape)
        lane = iota((size, width), 1)
        scale = weight[lo : lo + size, :]
        tile = jnp.zeros((size, width), F32)
        for r in range(rows):
            at = slice(r * width, (r + 1) * width)
            summed = sums[lo : lo + size, at]
            for d in away:
                summed = summed + part_in[d, lo : lo + size, at].astype(F32)
            value = ((number[0:1, at] * model[lo : lo + size, at] - summed) * scale).astype(BF16)
            total[lo : lo + size, at] = value
            value = value.astype(F32)
            ends = jnp.where(lane < STEPS, value, pltpu.roll(value, EDGE, 1))
            if r > 0:
                ends = pltpu.roll(ends, EDGE * r, 1)
            tile = jnp.where((lane >= EDGE * r) & (lane < EDGE * (r + 1)), ends, tile)
        side_out[lo : lo + size, :] = tile.astype(BF16)
        for s in range(2):
            only(1 - 2 * s, lambda: row_copy(h, s).start())
        for k in range(len(SIDES)):
            only(-SIDES[k][0], lambda: side_copy(h, k).start())

    def back(values):
        return lax.dot_general(values, jac[...], (((0,), (0,)), ((), ())), preferred_element_type=F32)

    def put_row(values, r):
        result = back(values)
        for j in range(chunks):
            field[j, r, EDGE : EDGE + width, :] = result[:, j * LANES : (j + 1) * LANES]

    @pl.loop(0, rows)
    def _(r):
        put_row(total[:, pl.ds(pl.multiple_of(r * width, width), width)], STEPS + r)

    for h in range(len(parts)):
        for k in range(len(SIDES)):
            only(SIDES[k][0], lambda: side_copy(h, k).wait_recv())
        for s in range(2):
            only(2 * s - 1, lambda: row_copy(h, s).wait_recv())

    lane = iota((height, width), 1)
    west_east = [
        jnp.where(lax.rem(lane, EDGE) < STEPS, side_in[k + 1].astype(F32), side_in[k].astype(F32))
        for k in (0, 2, 4)
    ]
    middle = pltpu.roll(west_east[0], STEPS * EDGE, 1)
    upper = pltpu.roll(west_east[1], width - (rows - STEPS) * EDGE, 1)
    lower = pltpu.roll(west_east[2], (rows + STEPS) * EDGE, 1)
    side = jnp.where(
        lane < STEPS * EDGE, upper, jnp.where(lane < (rows + STEPS) * EDGE, middle, lower)
    )
    result = back(side.astype(BF16))
    for j in range(chunks):
        for r in range(extent):
            piece = result[r * EDGE : (r + 1) * EDGE, j * LANES : (j + 1) * LANES]
            field[j, r, 0:EDGE, :] = piece
            field[j, r, EDGE + width :, :] = piece

    @pl.loop(0, STEPS)
    def _(r):
        at = pl.ds(pl.multiple_of(r * width, width), width)
        put_row(total_north[:, at], r)
        put_row(total_south[:, at], STEPS + rows + r)

    spread()

    @pl.loop(0, rows)
    def _(r):
        for j in range(chunks):
            at = pl.ds(j * step_rows + r, LANES, stride=rows)
            raw[0, at, :] = raw[0, at, :] + jnp.transpose(field[j, STEPS + r, EDGE : EDGE + width, :])

    store = pltpu.make_async_copy(raw.at[0, pl.ds(0, area), :], out, store_sem)
    store.start()

    for d in range(n_lat):
        for h in range(len(parts)):
            @pl.loop(1, n_lon)
            def _(i):
                block_copy(d, h, i).wait_send()
    for h in range(len(parts)):
        for d in away:
            part_copy(d, h).wait_send()
        for s in range(2):
            only(1 - 2 * s, lambda: row_copy(h, s).wait_send())
        for k in range(len(SIDES)):
            only(-SIDES[k][0], lambda: side_copy(h, k).wait_send())
    for a in range(2):
        for s in range(2):
            only(1 - 2 * s, lambda: band_copy(a, s).wait_send())
        for k in range(len(SIDES)):
            only(-SIDES[k][0], lambda: tile_copy(a, k).wait_send())
    store.wait()


def per_device(control, kappa, pc_obs, owner, columns, counts, jacobian, obs_weight):
    n_lat, n_lon = lax.axis_size("lat"), lax.axis_size("lon")
    fields, levels, rows, width = control.shape
    soundings, comps = pc_obs.shape[1:]
    planes = fields * levels
    cells = rows * width
    height = -(-(comps + HEAD) // 16) * 16
    chunks = -(-planes // LANES)
    extent, wide = rows + 2 * STEPS, width + 2 * EDGE
    half = -(-height // 32) * 16
    parts = ((0, half), (half, height - half))
    order = tuple(sorted(range(1, n_lat), key=lambda d: -min(d, n_lat - d))) + (0,)
    sent = pack(pc_obs, owner, columns, counts, n_lat * n_lon, height)
    sent = sent.reshape(n_lat, n_lon, CAP, height, soundings)
    room = (HEAD, height - HEAD - comps)
    jac = jnp.pad(jnp.transpose(jacobian), (room, (0, chunks * LANES - planes)))
    weight = jnp.pad(obs_weight[:, None], (room, (0, 0)))
    n_parts, n_sides = len(parts), len(SIDES)
    grid = pltpu.VMEM((chunks, extent, wide, LANES), F32)
    dma = pltpu.SemaphoreType.DMA
    result = pl.pallas_call(
        functools.partial(main_kernel, n_lat, n_lon, planes, parts, order),
        out_shape=jax.ShapeDtypeStruct((planes * rows, width), F32),
        in_specs=[pl.BlockSpec(memory_space=pl.ANY)] * 3
        + [pl.BlockSpec(memory_space=pltpu.VMEM)] * 2,
        out_specs=pl.BlockSpec(memory_space=pl.ANY),
        scratch_shapes=[
            pltpu.VMEM((n_lat, n_lon, CAP, height, soundings), BF16),
            pltpu.VMEM((n_lat - 1, height, cells), BF16),
            pltpu.VMEM((n_lat - 1, height, cells), BF16),
            pltpu.VMEM((height, cells), F32),
            pltpu.VMEM((8, cells), F32),
            pltpu.VMEM((height, cells), F32),
            grid, grid, grid, grid,
            pltpu.VMEM((2, chunks * LANES * rows, width), F32),
            pltpu.VMEM((2, rows, chunks, width, LANES), BF16),
            pltpu.VMEM((2, 2, STEPS, chunks, width, LANES), BF16),
            pltpu.VMEM((chunks, rows, EDGE, LANES), F32),
            pltpu.VMEM((2, chunks, rows * EDGE, LANES), BF16),
            pltpu.VMEM((2, n_sides, chunks, rows * EDGE, LANES), BF16),
            pltpu.VMEM((height, cells), BF16),
            pltpu.VMEM((height, STEPS * width), BF16),
            pltpu.VMEM((height, STEPS * width), BF16),
            pltpu.VMEM((height, width), BF16),
            pltpu.VMEM((n_sides, height, width), BF16),
            dma((2,)), dma((n_lat,)),
            dma((n_lat, n_parts, n_lon)), dma((n_lat, n_parts, n_lon)),
            dma((n_lat, n_parts)), dma((n_lat, n_parts)),
            dma((2, 2)), dma((2, 2)), dma((2, n_sides)), dma((2, n_sides)),
            dma((n_parts, 2)), dma((n_parts, 2)), dma((n_parts, n_sides)), dma((n_parts, n_sides)),
            dma,
        ],
        compiler_params=pltpu.CompilerParams(vmem_limit_bytes=60 * 2**20, has_side_effects=True),
    )(
        sent, control.reshape(planes * rows, width), kappa.reshape(planes * rows, width), jac, weight
    )
    return result.reshape(control.shape)


def solution(mesh):
    placed = (
        P(None, None, "lat", "lon"),
        P(None, None, "lat", "lon"),
        P(("lat", "lon"), None, None),
        P(("lat", "lon"), None),
        P(("lat", "lon"), None),
        P(("lat", "lon")),
        P(),
        P(),
    )
    return jax.shard_map(
        per_device,
        mesh=mesh,
        in_specs=placed,
        out_specs=P(None, None, "lat", "lon"),
        check_vma=False,
    )
```

time: 271 us -> 153 us (0.56)
  waiting for transfers between devices: 70.2 us -> 0 us
  Pallas kernels: 91.7 us -> 145 us
  local copies, waits for them, and re-layouts: 51 us -> 7.06 us
  other arithmetic: 30.8 us -> 0 us
  starting transfers between devices: 21.5 us -> 0 us
    pallas_call x4 -> x2, Pallas kernels: 91.7 us -> 145 us  [the longest x1 130 us: per_device(): pl.pallas_call(functools.partial(main_kernel, n_lat, n_lon, planes, parts...]
    all_to_all x1 -> x0, waiting for transfers between devices: 52.2 us -> none  [per_device(): lax.all_to_all(sent, ('lat', 'lon'), split_axis=0, concat_axis=0, tiled=T...]
    unnamed x36 -> x1, local copies, waits for them, and re-layouts: 25.5 us -> 2.58 us
    slice x14 -> x0, local copies, waits for them, and re-layouts: 20.9 us -> none  [the longest x5 10.9 us: rims(): head = main[:, :, :STEPS].reshape(planes, -1).astype(jnp.bfloat16)]
    concatenate x5 -> x0, other arithmetic: 18.2 us -> none  [the longest x2 12.4 us: side_tile(): return jnp.concatenate([parts[:, 0], gap, parts[:, 1]], axis=2)]
    ppermute x12 -> x0, waiting for transfers between devices: 17.9 us -> none  [the longest x3 8.35 us: rims(): lax.ppermute(core[:, -STEPS:].astype(jnp.bfloat16), 'lat', ring('lat', 1))]
    ppermute x12 -> x0, starting transfers between devices: 17.9 us -> none  [the longest x3 8.54 us: rims(): lax.ppermute(core[:, :STEPS].astype(jnp.bfloat16), 'lat', ring('lat', -1))]
    convert_element_type x5 -> x0, other arithmetic: 5.49 us -> none  [the longest x2 1.53 us: rims(): return (main, jnp.concatenate([east, west], axis=1).astype(core.dtype))]
  transfers between devices with their start and end apart: 13 -> 0, of which waited for: 5 -> 0; matrix products, arithmetic and copies ran while one was open for 25% -> 0% of each run, Pallas kernels for 18% -> 0%
where the time goes in v1:
time: 153 us; the launch traced here: 152 us
  Pallas kernels  145 us (95%)
  local copies, waits for them, and re-layouts  7.06 us (5%)
    pallas_call x1, Pallas kernels, per_device(): pl.pallas_call(functools.partial(main_kernel, n_lat, n_lon, planes, parts...  130 us
    pallas_call x1, Pallas kernels, pack(): pl.pallas_call(functools.partial(pack_kernel, group), out_shape=jax.Shape...  14.4 us

profile of v1, /device:TPU:1, one launch (start us, length us, event | category | flops | bytes accessed | tf_op | source)
XLA Modules:
  0.0 151.9 jit_solution(12292561168896235640)
XLA Ops:
  0.0 1.3 copy.10.counts_ref
  1.3 0.8 broadcast_in_dim.8
  2.1 0.7 pad.9.weight
  2.8 1.7 %pad.8.jac = bf16[304,384]{1,0:T(8,128)(2,1)} pad(bf16[300,360]{1,0:T(8,128)(2,1)} %bitcast.13, bf16[]{:T(256)} %constant.3.clone.1), padding=4_0x0_24 | pad | bytes 449474 | tf_op jit(solution)/shard_map/jit(_pad)/pad | solution.py:451
  4.5 14.4 %shard_map.82 = bf16[64,304,128]{2,1,0:T(8,128)(2,1)} custom-call(s32[32]{0:T(128)} %bitcast.15, bf16[300,32,128]{2,1,0:T(8,128)(2,1)} %bitcast.10, s32[32,128]{1,0:T(8,128)} %columns_ref.1, s32[32,1]{1,0:T(8,128)} %copy.10.counts_ref), custom_call_target="tpu_custom_call" | custom-call | tf_op jit(solution)/shard_map/pallas_call | solution.py:71
  18.9 130.5 %shard_map.83 = f32[2880,128]{1,0:T(8,128)} custom-call(bf16[4,8,2,304,128]{4,3,2,1,0:T(8,128)(2,1)} %bitcast.8, f32[2880,128]{1,0:T(8,128)} %bitcast.11, f32[2880,128]{1,0:T(8,128)} %bitcast.12, bf16[304,384]{1,0:T(8,128)(2,1)} %pad.8.jac, f32[304,1]{1,0:T(8,128)} %pad.9.weight), custom_call_target="tpu_custom_call" | custom-call | tf_op jit(solution)/shard_map/pallas_call | solution.py:456
  149.4 2.6 %copy.13 = f32[4,90,8,128]{3,2,1,0:T(8,128)} copy(f32[4,90,8,128]{3,2,1,0:T(8,128)} %bitcast.9) | data formatting | bytes 2949120

commit v2 on v1

v2 whole, which is shorter than its diff:
```python
import functools

import jax
import jax.numpy as jnp
from jax import lax
from jax.experimental import pallas as pl
from jax.experimental.pallas import tpu as pltpu
from jax.sharding import PartitionSpec as P

CAP = 2
STEPS = 4
LANES = 128
GROUP = 16
EDGE = 8
TAIL = 4
COUNT_BASE = 64
TILE = 256
MESH = pl.DeviceIdType.MESH
F32 = jnp.float32
BF16 = jnp.bfloat16
SIDES = ((0, -1), (0, 1), (-1, -1), (-1, 1), (1, -1), (1, 1))


def iota(shape, dim):
    return lax.broadcasted_iota(jnp.int32, shape, dim)


def to_column(row, size):
    shape = (size, row.shape[1])
    return jnp.sum(jnp.where(iota(shape, 0) == iota(shape, 1), row, 0.0), axis=1, keepdims=True)


def digits(columns, counts):
    low = jnp.bitwise_and(columns, 31)
    valid = iota(columns.shape, 1).astype(F32) < counts
    high = jnp.where(valid, jnp.right_shift(columns - low, 5) + 1, 0)
    zero = jnp.zeros(columns.shape, F32)
    return [zero + 1.0, high.astype(F32), low.astype(F32), zero]


def pack_kernel(group, owner_ref, obs_ref, columns_ref, counts_ref, out_ref, wide, source):
    blocks = columns_ref.shape[0]
    comps = obs_ref.shape[0]
    height = out_ref.shape[1]
    slots = source.shape[0]

    @pl.when(pl.program_id(0) == 0)
    def _():
        @pl.loop(0, slots)
        def _(t):
            source[t] = -1

        @pl.loop(0, blocks)
        def _(b):
            first = owner_ref[b] * CAP
            source[jnp.where(source[first] < 0, first, first + 1)] = b

        @pl.loop(0, comps, unroll=4)
        def _(c):
            wide[pl.ds(pl.multiple_of(c * blocks, blocks), blocks), :] = obs_ref[c].astype(F32)

        for k, row in enumerate(digits(columns_ref[...], to_column(counts_ref[...].astype(F32), blocks))):
            wide[(comps + k) * blocks : (comps + k + 1) * blocks, :] = row

    for g in range(group):
        block = source[pl.program_id(0) * group + g]
        rows = wide[pl.ds(jnp.maximum(block, 0), height, stride=blocks), :]
        out_ref[g] = jnp.where(block < 0, 0.0, rows).astype(BF16)


def pack(obs, owner, columns, counts, peers, height):
    comps, blocks, soundings = obs.shape
    slots = peers * CAP
    group = 8
    return pl.pallas_call(
        functools.partial(pack_kernel, group),
        out_shape=jax.ShapeDtypeStruct((slots, height, soundings), BF16),
        grid_spec=pltpu.PrefetchScalarGridSpec(
            num_scalar_prefetch=1,
            grid=(slots // group,),
            in_specs=[
                pl.BlockSpec((comps, blocks, soundings), lambda i, s: (0, 0, 0)),
                pl.BlockSpec((blocks, soundings), lambda i, s: (0, 0)),
                pl.BlockSpec((1, blocks), lambda i, s: (0, 0)),
            ],
            out_specs=pl.BlockSpec((group, height, soundings), lambda i, s: (i, 0, 0)),
            scratch_shapes=[
                pltpu.VMEM((height * blocks, soundings), F32),
                pltpu.SMEM((slots,), jnp.int32),
            ],
        ),
        compiler_params=pltpu.CompilerParams(vmem_limit_bytes=56 * 2**20),
    )(owner[:, 0], obs, columns, counts[None, :])


def main_kernel(n_lat, n_lon, planes, parts, packed, *refs):
    source, control, kappa, jac_in, weight_in, owner, counts, columns, out, *refs = refs
    sent, obs, codes = (source, None, None) if packed else refs[:3]
    (
        recv, ring, part_out, part_in, sums, number, model, jac, scale,
        field, coef, east, raw, band_out, band_in, tile_f, tile_out, tile_in,
        total, total_north, total_south, side_out, side_in,
        load_sem, own_sem, blk_send, blk_recv, part_send, part_recv,
        band_send, band_recv, tile_send, tile_recv, row_send, row_recv, side_send, side_recv, store_sem,
    ) = refs if packed else refs[3:]
    lat, lon = lax.axis_index("lat"), lax.axis_index("lon")
    height, cells = sums.shape
    comps = jac_in.shape[0]
    chunks, extent, wide, _ = field.shape
    rows = extent - 2 * STEPS
    width = wide - 2 * EDGE
    area = planes * rows
    step_rows = LANES * rows
    slots = n_lon * CAP
    band_rows = STEPS * EDGE

    def plane_of(k):
        mirrored = lat >= n_lat - n_lat // 2
        z = jnp.where(mirrored, n_lat - 1 - lat, lat)
        o = jnp.where(k < n_lat - 1 - z, n_lat - 1 - k, k - (n_lat - 1 - z))
        return jnp.where(mirrored, n_lat - 1 - o, o)

    def remote(src, dst, send, recv_, to):
        return pltpu.make_async_remote_copy(
            src_ref=src, dst_ref=dst, send_sem=send, recv_sem=recv_, device_id=to, device_id_type=MESH
        )

    def around(step):
        return lax.rem(lon + step + n_lon, n_lon)

    def has(step):
        return (lat + step >= 0) & (lat + step < n_lat)

    def only(step, act):
        if step == 0:
            act()
        else:
            pl.when(has(step))(act)

    def slot_of(k):
        return plane_of(k) if packed else k

    def block_copy(k, h, i):
        lo, size = parts[h]
        return remote(
            sent.at[slot_of(k), around(i), :, pl.ds(lo, size), :], recv.at[k, i, :, pl.ds(lo, size), :],
            blk_send.at[k, h, i], blk_recv.at[k, h, i], (lat, around(i)),
        )

    def own_copy(k, h):
        lo, size = parts[h]
        return pltpu.make_async_copy(
            sent.at[slot_of(k), lon, :, pl.ds(lo, size), :],
            recv.at[k, 0, :, pl.ds(lo, size), :], own_sem.at[k, h],
        )

    def part_copy(k, h, slot, to):
        lo, size = parts[h]
        return remote(
            part_out.at[k, pl.ds(lo, size), :], part_in.at[slot, pl.ds(lo, size), :],
            part_send.at[k, h], part_recv.at[slot, h], (to, lon),
        )

    def part_sent(k, h):
        o = plane_of(k)
        north = o < lat
        slot = jnp.where(north & (o == lat - 1), n_lat, o)
        return part_copy(k, h, slot, jnp.where(north, lat - 1, lat + 1))

    def band_copy(a, s):
        return remote(
            band_out.at[a, pl.ds((1 - s) * (rows - STEPS), STEPS)], band_in.at[a, s],
            band_send.at[a, s], band_recv.at[a, s], (lat + (1 - 2 * s), lon),
        )

    def peer(k):
        return (lat - SIDES[k][0], around(-SIDES[k][1]))

    def side_span(k):
        step = SIDES[k][0]
        if step == 0:
            return pl.ds(0, rows * EDGE)
        return pl.ds((rows * EDGE - band_rows) if step < 0 else 0, band_rows)

    def tile_copy(a, k):
        span = side_span(k)
        return remote(
            tile_out.at[a, :, span, :], tile_in.at[a, k, :, span, :],
            tile_send.at[a, k], tile_recv.at[a, k], peer(k),
        )

    def row_copy(h, s):
        lo, size = parts[h]
        span = STEPS * width
        return remote(
            total.at[pl.ds(lo, size), pl.ds((1 - s) * (rows * width - span), span)],
            (total_north if s == 0 else total_south).at[pl.ds(lo, size), :],
            row_send.at[h, s], row_recv.at[h, s], (lat + (1 - 2 * s), lon),
        )

    def side_copy(k):
        span = side_span(k)
        return remote(
            side_out.at[span, :], side_in.at[k, span, :], side_send.at[k], side_recv.at[k], peer(k)
        )

    barrier = pltpu.get_barrier_semaphore()

    @pl.loop(1, n_lon)
    def _(i):
        pl.semaphore_signal(barrier, inc=1, device_id=(lat, around(i)), device_id_type=MESH)

    for step in (-1, 1):
        def greet():
            for side in (-1, 0, 1):
                pl.semaphore_signal(
                    barrier, inc=1, device_id=(lat + step, around(side)), device_id_type=MESH
                )

        only(step, greet)

    loads = [
        pltpu.make_async_copy(ref, raw.at[a, pl.ds(0, area), :], load_sem.at[a])
        for a, ref in enumerate((control, kappa))
    ]
    if not packed:
        obs_load = pltpu.make_async_copy(source, obs, load_sem.at[2])
        obs_load.start()
    for load in loads:
        load.start()

    if not packed:
        blocks = columns.shape[0]
        names = owner[...].astype(F32)
        square = (blocks, blocks)
        before = (to_column(names, blocks) == names) & (iota(square, 0) < iota(square, 1))
        place = names * CAP + jnp.sum(jnp.where(before, 1.0, 0.0), axis=0, keepdims=True)
        lined = (blocks, GROUP * blocks)
        comb = jnp.where(lax.rem(iota(lined, 1), blocks) == iota(lined, 0), 1.0, 0.0).astype(BF16)
        place = jnp.broadcast_to(place, (16, blocks)).astype(BF16)
        place = jnp.dot(place, comb, preferred_element_type=F32)[0:1].astype(jnp.int32)
        code = digits(columns[...], to_column(counts[...].astype(F32), blocks))
        codes[...] = jnp.concatenate(code, axis=0).astype(BF16)

    def pack_round(k, h):
        shape = (slots * GROUP, GROUP * blocks)
        at = plane_of(k) * slots + jnp.right_shift(iota(shape, 0), 4)
        hit = (place == at) & (jnp.bitwise_and(iota(shape, 0), GROUP - 1) == iota(shape, 1) // blocks)
        pick = jnp.where(hit, 1.0, 0.0).astype(BF16)
        lo, size = parts[h]
        span = GROUP * blocks

        def put(first, values):
            for t in range(slots):
                part = values[t * GROUP : (t + 1) * GROUP].astype(BF16)
                sent[k, t // CAP, t % CAP, pl.ds(first, GROUP), :] = part

        pairs = (min(lo + size, height - GROUP) - lo) // (2 * GROUP)

        @pl.loop(0, pairs)
        def _(p):
            first = pl.multiple_of(lo + p * 2 * GROUP, GROUP)
            start = pl.multiple_of(first * blocks, span)
            both = jnp.concatenate([obs[pl.ds(start, span), :], obs[pl.ds(start + span, span), :]], axis=1)
            values = jnp.dot(pick, both, preferred_element_type=F32)
            put(first, values[:, :LANES])
            put(pl.multiple_of(first + GROUP, GROUP), values[:, LANES:])

        if lo + size == height:
            last = jnp.concatenate([obs[(height - GROUP) * blocks :, :], codes[...]], axis=0)
            put(height - GROUP, jnp.dot(pick, last, preferred_element_type=F32))

    def send_round(k, h):
        if not packed:
            pack_round(k, h)
        if k == 0 and h == 0:
            pl.semaphore_wait(
                barrier, n_lon - 1 + 3 * (has(-1).astype(jnp.int32) + has(1).astype(jnp.int32))
            )

        @pl.loop(1, n_lon)
        def _(i):
            block_copy(k, h, i).start()

        own_copy(k, h).start()

    if not packed:
        obs_load.wait()
    send_round(0, 0)

    sub = iota((EDGE, LANES), 0)
    for a, grid in ((1, coef), (0, field)):
        loads[a].wait()
        if chunks * step_rows > area:
            raw[a, area:, :] = jnp.zeros((chunks * step_rows - area, width), F32)

        @pl.loop(0, rows)
        def _(r):
            for j in range(chunks):
                turned = jnp.transpose(raw[a, pl.ds(j * step_rows + r, LANES, stride=rows), :])
                grid[j, STEPS + r, EDGE : EDGE + width, :] = turned
                band_out[a, r, j] = turned.astype(BF16)
                tile_f[j, r] = jnp.where(sub < STEPS, turned[:EDGE], turned[width - EDGE :])

        tile_out[a] = tile_f[...].reshape(chunks, rows * EDGE, LANES).astype(BF16)
        for s in range(2):
            only(1 - 2 * s, lambda: band_copy(a, s).start())
        for k in range(len(SIDES)):
            only(-SIDES[k][0], lambda: tile_copy(a, k).start())
        if a == 1:
            send_round(0, 1)

    for k in range(1, n_lat):
        for h in range(len(parts)):
            send_round(k, h)

    matrix = jac_in[...].astype(F32)
    matrix = jnp.concatenate([matrix, jnp.zeros((height - comps, planes), F32)], axis=0)
    if chunks * LANES > planes:
        matrix = jnp.concatenate([matrix, jnp.zeros((height, chunks * LANES - planes), F32)], axis=1)
    jac[...] = matrix.astype(BF16)
    scale[...] = jnp.broadcast_to(to_column(weight_in[...], height), scale.shape)

    def pad_line(h):
        return comps - parts[h][0]

    def lanes(n):
        return pl.ds(pl.multiple_of(n * TILE, TILE), TILE)

    def reduce(k, h):
        lo, size = parts[h]

        @pl.loop(1, n_lon)
        def _(i):
            block_copy(k, h, i).wait_recv()

        own_copy(k, h).wait()
        base = height - GROUP
        first = comps - base
        heads = [recv[k, i, c, base:height, :].astype(F32) for i in range(n_lon) for c in range(CAP)]
        code = jnp.concatenate(
            [(x[first + 1 : first + 2] - 1.0) * 32.0 + x[first + 2 : first + 3] for x in heads], axis=1
        ).astype(jnp.int32)

        @pl.loop(0, cells // TILE)
        def _(n):
            values = jnp.concatenate(
                [recv[k, i, c, lo : lo + size, :] for i in range(n_lon) for c in range(CAP)], axis=1
            )
            hot = jnp.where(iota((TILE, code.shape[1]), 0) == code - n * TILE, 1.0, 0.0).astype(BF16)
            part = lax.dot_general(values, hot, (((1,), (1,)), ((), ())), preferred_element_type=F32)
            if k == n_lat - 1:
                sums[lo : lo + size, lanes(n)] = part
                if h == 0:
                    line = pad_line(h)
                    number[:, lanes(n)] = jnp.broadcast_to(part[line : line + 1], (8, TILE))
            else:
                ring[k % 2, lo : lo + size, lanes(n)] = part

        if k < n_lat - 1:
            pl.when(jnp.logical_not(has(-1) & has(1)))(lambda: emit(k, h, False))

    def emit(k, h, joined):
        lo, size = parts[h]
        o = plane_of(k)
        if joined:
            part_copy(k, h, o, lat).wait_recv()

        @pl.loop(0, cells // TILE)
        def _(n):
            value = ring[k % 2, lo : lo + size, lanes(n)]
            if h == 0:
                line = pad_line(h)
                count = value[line : line + 1]
            if joined:
                more = part_in[o, lo : lo + size, lanes(n)].astype(F32)
                value = value + more
                if h == 0:
                    count = count + more[line : line + 1] + more[line + 1 : line + 2] * COUNT_BASE
            if h == 0:
                high = jnp.floor(count * (1.0 / COUNT_BASE))
                at = iota(value.shape, 0)
                value = jnp.where(at == line, count - high * COUNT_BASE, jnp.where(at == line + 1, high, value))
            part_out[k, lo : lo + size, lanes(n)] = value.astype(BF16)

        part_sent(k, h).start()

    def join(k):
        for h in range(len(parts)):
            pl.when(has(-1) & has(1))(lambda: emit(k, h, True))

    def fill_edges(a, grid):
        def band(s):
            first = (rows + STEPS) * s

            def arrived():
                band_copy(a, s).wait_recv()
                for r in range(STEPS):
                    for j in range(chunks):
                        grid[j, first + r, EDGE : EDGE + width, :] = band_in[a, s, r, j].astype(F32)

            def closed():
                for r in range(STEPS):
                    for j in range(chunks):
                        grid[j, first + r] = jnp.zeros((wide, LANES), F32)

            pl.when(has(2 * s - 1))(arrived)
            pl.when(jnp.logical_not(has(2 * s - 1)))(closed)

        for s in range(2):
            band(s)

        def sides(west, count, place, source_row):
            tile_copy(a, west).wait_recv()
            tile_copy(a, west + 1).wait_recv()
            span = slice(source_row * EDGE, (source_row + count) * EDGE)
            shape = (chunks, count, EDGE, LANES)
            both = [tile_in[a, k, :, span, :].astype(F32).reshape(shape) for k in (west, west + 1)]
            for j in range(chunks):
                for r in range(count):
                    tile = jnp.where(sub < STEPS, both[1][j, r], both[0][j, r])
                    grid[j, place + r, 0:EDGE, :] = tile
                    grid[j, place + r, EDGE + width :, :] = tile

        sides(0, rows, STEPS, 0)
        only(-1, lambda: sides(2, STEPS, 0, rows - STEPS))
        only(1, lambda: sides(4, STEPS, rows + STEPS, 0))

    def spread(j):
        for step in range(STEPS):
            first, last = step + 1, extent - 1 - step
            here = field[j, first]
            above = coef[j, first - 1] * (here - field[j, first - 1])

            def line(r, carry):
                here, above = carry
                below = field[j, r + 1]
                down = coef[j, r] * (below - here)
                along = east[j, r] * (pltpu.roll(here, wide - 1, 0) - here)
                field[j, r] = here + (down - above) + (along - pltpu.roll(along, 1, 0))
                return below, down

            lax.fori_loop(first, last, line, (here, above))

    def make_state():
        fill_edges(1, coef)

        @pl.loop(0, chunks)
        def _(j):
            @pl.loop(0, extent - 1)
            def _(r):
                here = coef[j, r]
                east[j, r] = here * pltpu.roll(here, wide - 1, 0)
                coef[j, r] = here * coef[j, r + 1]

        fill_edges(0, field)
        pl.loop(0, chunks)(spread)

        @pl.loop(0, rows)
        def _(r):
            state = jnp.concatenate(
                [field[j, STEPS + r, EDGE : EDGE + width, :].astype(BF16) for j in range(chunks)], axis=1
            )
            model[:, pl.ds(pl.multiple_of(r * width, width), width)] = lax.dot_general(
                jac[...], state, (((1,), (1,)), ((), ())), preferred_element_type=F32
            )

    for k in range(n_lat - 1):
        for h in range(len(parts)):
            reduce(k, h)
        if k > 0:
            join(k - 1)
        if k == min(1, n_lat - 2):
            make_state()
    join(n_lat - 2)
    for h in range(len(parts)):
        reduce(n_lat - 1, h)

    for s, ref in enumerate((total_north, total_south)):
        def blank():
            ref[...] = jnp.zeros(ref.shape, BF16)
            side_in[2 + 2 * s] = jnp.zeros(side_in.shape[1:], BF16)
            side_in[3 + 2 * s] = jnp.zeros(side_in.shape[1:], BF16)

        pl.when(jnp.logical_not(has(2 * s - 1)))(blank)

    def add_part(slot, h):
        lo, size = parts[h]
        part_copy(0, h, slot, lat).wait_recv()

        @pl.loop(0, cells // TILE)
        def _(n):
            more = part_in[slot, lo : lo + size, lanes(n)].astype(F32)
            sums[lo : lo + size, lanes(n)] = sums[lo : lo + size, lanes(n)] + more
            if h == 0:
                line = pad_line(h)
                count = more[line : line + 1] + more[line + 1 : line + 2] * COUNT_BASE
                number[:, lanes(n)] = number[:, lanes(n)] + count

    for h, (lo, size) in enumerate(parts):
        only(-1, lambda: add_part(lat, h))
        only(1, lambda: add_part(n_lat, h))
        for r in range(rows):
            at = slice(r * width, (r + 1) * width)
            value = number[0:1, at] * model[lo : lo + size, at] - sums[lo : lo + size, at]
            total[lo : lo + size, at] = (value * scale[lo : lo + size, :]).astype(BF16)
        for s in range(2):
            only(1 - 2 * s, lambda: row_copy(h, s).start())

    ends = (rows * EDGE, cells)
    line = iota(ends, 0)
    spot = jnp.bitwise_and(line, EDGE - 1)
    spot = (line // EDGE) * width + jnp.where(spot < STEPS, spot, spot + width - EDGE)
    ends = jnp.where(iota(ends, 1) == spot, 1.0, 0.0).astype(BF16)
    side_out[...] = lax.dot_general(
        ends, total[...], (((1,), (1,)), ((), ())), preferred_element_type=F32
    ).astype(BF16)
    for k in range(len(SIDES)):
        only(-SIDES[k][0], lambda: side_copy(k).start())

    def put_row(values, r):
        result = lax.dot_general(values, jac[...], (((0,), (0,)), ((), ())), preferred_element_type=F32)
        for j in range(chunks):
            field[j, r, EDGE : EDGE + width, :] = result[:, j * LANES : (j + 1) * LANES]

    @pl.loop(0, rows)
    def _(r):
        put_row(total[:, pl.ds(pl.multiple_of(r * width, width), width)], STEPS + r)

    for k in range(len(SIDES)):
        only(SIDES[k][0], lambda: side_copy(k).wait_recv())

    def west_east(west, span):
        values = [side_in[k, span, :].astype(F32) for k in (west, west + 1)]
        left = jnp.bitwise_and(iota(values[0].shape, 0), EDGE - 1) < STEPS
        return jnp.where(left, values[1], values[0])

    side = jnp.concatenate(
        [
            west_east(2, slice((rows - STEPS) * EDGE, rows * EDGE)),
            west_east(0, slice(0, rows * EDGE)),
            west_east(4, slice(0, band_rows)),
        ],
        axis=0,
    ).astype(BF16)
    result = jnp.dot(side, jac[...], preferred_element_type=F32)
    for j in range(chunks):
        for r in range(extent):
            piece = result[r * EDGE : (r + 1) * EDGE, j * LANES : (j + 1) * LANES]
            field[j, r, 0:EDGE, :] = piece
            field[j, r, EDGE + width :, :] = piece

    for h in range(len(parts)):
        for s in range(2):
            only(2 * s - 1, lambda: row_copy(h, s).wait_recv())

    @pl.loop(0, STEPS)
    def _(r):
        at = pl.ds(pl.multiple_of(r * width, width), width)
        put_row(total_north[:, at], r)
        put_row(total_south[:, at], STEPS + rows + r)

    stores = []
    for j in range(chunks):
        spread(j)

        @pl.loop(0, rows)
        def _(r):
            at = pl.ds(j * step_rows + r, LANES, stride=rows)
            raw[0, at, :] = raw[0, at, :] + jnp.transpose(field[j, STEPS + r, EDGE : EDGE + width, :])

        span = pl.ds(j * step_rows, min(step_rows, area - j * step_rows))
        stores.append(pltpu.make_async_copy(raw.at[0, span, :], out.at[span, :], store_sem.at[j]))
        stores[-1].start()

    for k in range(n_lat):
        for h in range(len(parts)):
            @pl.loop(1, n_lon)
            def _(i):
                block_copy(k, h, i).wait_send()
    for h in range(len(parts)):
        for k in range(n_lat - 1):
            part_sent(k, h).wait_send()
        for s in range(2):
            only(1 - 2 * s, lambda: row_copy(h, s).wait_send())
    for k in range(len(SIDES)):
        only(-SIDES[k][0], lambda: side_copy(k).wait_send())
    for a in range(2):
        for s in range(2):
            only(1 - 2 * s, lambda: band_copy(a, s).wait_send())
        for k in range(len(SIDES)):
            only(-SIDES[k][0], lambda: tile_copy(a, k).wait_send())
    for store in stores:
        store.wait()


def per_device(control, kappa, pc_obs, owner, columns, counts, jacobian, obs_weight):
    n_lat, n_lon = lax.axis_size("lat"), lax.axis_size("lon")
    fields, levels, rows, width = control.shape
    blocks, soundings, comps = pc_obs.shape
    planes = fields * levels
    cells = rows * width
    height = comps + TAIL
    chunks = -(-planes // LANES)
    extent, wide = rows + 2 * STEPS, width + 2 * EDGE
    half = -(-height // 64) * 32
    parts = ((half, height - half), (0, half))
    obs = jnp.transpose(pc_obs, (2, 0, 1))
    slots_shape = (n_lat, n_lon, CAP, height, soundings)
    packed = blocks * GROUP > 1024
    if packed:
        source = pack(obs, owner, columns, counts, n_lat * n_lon, height).reshape(slots_shape)
        extra = []
    else:
        source = obs.reshape(comps * blocks, soundings)
        extra = [
            pltpu.VMEM(slots_shape, BF16),
            pltpu.VMEM(source.shape, BF16),
            pltpu.VMEM((TAIL * blocks, soundings), BF16),
        ]
    n_parts, n_sides = len(parts), len(SIDES)
    grid = pltpu.VMEM((chunks, extent, wide, LANES), F32)
    dma = pltpu.SemaphoreType.DMA
    result = pl.pallas_call(
        functools.partial(main_kernel, n_lat, n_lon, planes, parts, packed),
        out_shape=jax.ShapeDtypeStruct((planes * rows, width), F32),
        in_specs=[pl.BlockSpec(memory_space=pl.ANY)] * 3
        + [pl.BlockSpec(memory_space=pltpu.VMEM)] * 5,
        out_specs=pl.BlockSpec(memory_space=pl.ANY),
        scratch_shapes=extra
        + [
            pltpu.VMEM(slots_shape, BF16),
            pltpu.VMEM((2, height, cells), F32),
            pltpu.VMEM((n_lat - 1, height, cells), BF16),
            pltpu.VMEM((n_lat + 1, height, cells), BF16),
            pltpu.VMEM((height, cells), F32),
            pltpu.VMEM((8, cells), F32),
            pltpu.VMEM((height, cells), F32),
            pltpu.VMEM((height, chunks * LANES), BF16),
            pltpu.VMEM((height, LANES), F32),
            grid, grid, grid,
            pltpu.VMEM((2, chunks * LANES * rows, width), F32),
            pltpu.VMEM((2, rows, chunks, width, LANES), BF16),
            pltpu.VMEM((2, 2, STEPS, chunks, width, LANES), BF16),
            pltpu.VMEM((chunks, rows, EDGE, LANES), F32),
            pltpu.VMEM((2, chunks, rows * EDGE, LANES), BF16),
            pltpu.VMEM((2, n_sides, chunks, rows * EDGE, LANES), BF16),
            pltpu.VMEM((height, cells), BF16),
            pltpu.VMEM((height, STEPS * width), BF16),
            pltpu.VMEM((height, STEPS * width), BF16),
            pltpu.VMEM((rows * EDGE, height), BF16),
            pltpu.VMEM((n_sides, rows * EDGE, height), BF16),
            dma((3,)), dma((n_lat, n_parts)),
            dma((n_lat, n_parts, n_lon)), dma((n_lat, n_parts, n_lon)),
            dma((n_lat, n_parts)), dma((n_lat + 1, n_parts)),
            dma((2, 2)), dma((2, 2)), dma((2, n_sides)), dma((2, n_sides)),
            dma((n_parts, 2)), dma((n_parts, 2)), dma((n_sides,)), dma((n_sides,)),
            dma((chunks,)),
        ],
        compiler_params=pltpu.CompilerParams(
            vmem_limit_bytes=62 * 2**20, has_side_effects=True, collective_id=0
        ),
    )(
        source, control.reshape(planes * rows, width), kappa.reshape(planes * rows, width),
        jnp.transpose(jacobian), obs_weight[None, :], owner.reshape(1, blocks), counts[None, :], columns,
    )
    return result.reshape(control.shape)


def solution(mesh):
    placed = (
        P(None, None, "lat", "lon"),
        P(None, None, "lat", "lon"),
        P(("lat", "lon"), None, None),
        P(("lat", "lon"), None),
        P(("lat", "lon"), None),
        P(("lat", "lon")),
        P(),
        P(),
    )
    return jax.shard_map(
        per_device,
        mesh=mesh,
        in_specs=placed,
        out_specs=P(None, None, "lat", "lon"),
        check_vma=False,
    )
```

time: 153 us -> 94.5 us (0.62)
  Pallas kernels: 145 us -> 90.4 us
  local copies, waits for them, and re-layouts: 7.06 us -> 3.82 us
    pallas_call x1, Pallas kernels: 130 us -> 90.4 us  [per_device(): pl.pallas_call(functools.partial(main_kernel, n_lat, n_lon, planes, parts...]
    pallas_call x1 -> x0, Pallas kernels: 14.4 us -> none  [pack(): pl.pallas_call(functools.partial(pack_kernel, group), out_shape=jax.Shape...]
    pad x2 -> x0, local copies, waits for them, and re-layouts: 2.38 us -> none  [the longest x1 1.69 us: per_device(): jac = jnp.pad(jnp.transpose(jacobian), (room, (0, chunks * LANES - planes)))]
where the time goes in v2:
time: 94.5 us; the launch traced here: 94.3 us
  Pallas kernels  90.4 us (96%)
  local copies, waits for them, and re-layouts  3.82 us (4%)
    pallas_call x1, Pallas kernels, per_device(): pl.pallas_call(functools.partial(main_kernel, n_lat, n_lon, planes, parts...  90.4 us
    unnamed x1, local copies, waits for them, and re-layouts  2.58 us

profile of v2, /device:TPU:1, one launch (start us, length us, event | category | flops | bytes accessed | tf_op | source)
XLA Modules:
  0.0 94.3 jit_solution(18141609344677702734)
XLA Ops:
  0.0 1.2 %broadcast_in_dim.6.refs_4_ = f32[1,300]{1,0:T(1,128)} reshape(f32[300]{0:T(512)} %param.15) | data formatting | bytes 2400 | tf_op jit(solution)/shard_map/broadcast_in_dim | solution.py:665
  1.2 90.4 %shard_map.82 = f32[2880,128]{1,0:T(8,128)} custom-call(bf16[9600,128]{1,0:T(8,128)(2,1)} %bitcast.10, f32[2880,128]{1,0:T(8,128)} %bitcast.11, f32[2880,128]{1,0:T(8,128)} %bitcast.12, bf16[300,360]{1,0:T(8,128)(2,1)} %bitcast.13, f32[1,300]{1,0:T(1,128)} %broadcast_in_dim.6.refs_4_, s32[1,32]{1,0:T(1,128)} %bitcast.14, s32[1,32]{1,0:T(1,128)} %bitcast.15, ...), custom_call_target="tpu_custom_call" | custom-call | tf_op jit(solution)/shard_map/pallas_call | solution.py:624
  91.7 2.6 %copy.10 = f32[4,90,8,128]{3,2,1,0:T(8,128)} copy(f32[4,90,8,128]{3,2,1,0:T(8,128)} %bitcast.9) | data formatting | bytes 2949120

commit v3 on v2

--- a/solution.py
+++ b/solution.py
@@ -94,11 +94,13 @@
 
 
 def main_kernel(n_lat, n_lon, planes, parts, packed, *refs):
-    source, control, kappa, jac_in, weight_in, owner, counts, columns, out, *refs = refs
+    source, control, kappa, *small_in, out = refs[:9]
+    small, refs = refs[9:14], refs[14:]
+    jac_in, weight_in, owner, counts, columns = small
     sent, obs, codes = (source, None, None) if packed else refs[:3]
     (
         recv, ring, part_out, part_in, sums, number, model, jac, scale,
-        field, coef, east, raw, band_out, band_in, tile_f, tile_out, tile_in,
+        field, coef, east, raw, band_out, band_in, band_f, tile_f, tile_out, tile_in,
         total, total_north, total_south, side_out, side_in,
         load_sem, own_sem, blk_send, blk_recv, part_send, part_recv,
         band_send, band_recv, tile_send, tile_recv, row_send, row_recv, side_send, side_recv, store_sem,
@@ -169,7 +171,7 @@
 
     def band_copy(a, s):
         return remote(
-            band_out.at[a, pl.ds((1 - s) * (rows - STEPS), STEPS)], band_in.at[a, s],
+            band_out.at[a, 1 - s], band_in.at[a, s],
             band_send.at[a, s], band_recv.at[a, s], (lat + (1 - 2 * s), lon),
         )
 
@@ -204,6 +206,22 @@
             side_out.at[span, :], side_in.at[k, span, :], side_send.at[k], side_recv.at[k], peer(k)
         )
 
+    loads = [
+        pltpu.make_async_copy(ref, raw.at[a, pl.ds(0, area), :], load_sem.at[a])
+        for a, ref in enumerate((control, kappa))
+    ]
+    small_loads = [
+        pltpu.make_async_copy(ref, to, load_sem.at[3 + n]) for n, (ref, to) in enumerate(zip(small_in, small))
+    ]
+    loads[1].start()
+    loads[0].start()
+    for load in small_loads[1:]:
+        load.start()
+    if not packed:
+        obs_load = pltpu.make_async_copy(source, obs, load_sem.at[2])
+        obs_load.start()
+    small_loads[0].start()
+
     barrier = pltpu.get_barrier_semaphore()
 
     @pl.loop(1, n_lon)
@@ -219,15 +237,25 @@
 
         only(step, greet)
 
-    loads = [
-        pltpu.make_async_copy(ref, raw.at[a, pl.ds(0, area), :], load_sem.at[a])
-        for a, ref in enumerate((control, kappa))
-    ]
-    if not packed:
-        obs_load = pltpu.make_async_copy(source, obs, load_sem.at[2])
-        obs_load.start()
-    for load in loads:
-        load.start()
+    sub = iota((EDGE, LANES), 0)
+    for a in (1, 0):
+        loads[a].wait()
+        if chunks * step_rows > area:
+            raw[a, area:, :] = jnp.zeros((chunks * step_rows - area, width), F32)
+        pairs = raw[a, 0:area, :].reshape(planes // 2, 2, rows, width)
+        even, odd = pairs[:, 0], pairs[:, 1]
+        upper = iota(even.shape, 1) < STEPS
+        band_out[a, 0] = jnp.where(upper, even, pltpu.roll(odd, STEPS, 1)).reshape(area // 2, width).astype(BF16)
+        band_out[a, 1] = jnp.where(upper, pltpu.roll(even, STEPS, 1), odd).reshape(area // 2, width).astype(BF16)
+        if a == 1:
+            pl.semaphore_wait(
+                barrier, n_lon - 1 + 3 * (has(-1).astype(jnp.int32) + has(1).astype(jnp.int32))
+            )
+        for s in range(2):
+            only(1 - 2 * s, lambda: band_copy(a, s).start())
+
+    for load in small_loads[1:]:
+        load.wait()
 
     if not packed:
         blocks = columns.shape[0]
@@ -273,10 +301,6 @@
     def send_round(k, h):
         if not packed:
             pack_round(k, h)
-        if k == 0 and h == 0:
-            pl.semaphore_wait(
-                barrier, n_lon - 1 + 3 * (has(-1).astype(jnp.int32) + has(1).astype(jnp.int32))
-            )
 
         @pl.loop(1, n_lon)
         def _(i):
@@ -286,40 +310,32 @@
 
     if not packed:
         obs_load.wait()
-    send_round(0, 0)
-
-    sub = iota((EDGE, LANES), 0)
+    for h in range(len(parts)):
+        send_round(0, h)
+
     for a, grid in ((1, coef), (0, field)):
-        loads[a].wait()
-        if chunks * step_rows > area:
-            raw[a, area:, :] = jnp.zeros((chunks * step_rows - area, width), F32)
-
         @pl.loop(0, rows)
         def _(r):
             for j in range(chunks):
                 turned = jnp.transpose(raw[a, pl.ds(j * step_rows + r, LANES, stride=rows), :])
                 grid[j, STEPS + r, EDGE : EDGE + width, :] = turned
-                band_out[a, r, j] = turned.astype(BF16)
                 tile_f[j, r] = jnp.where(sub < STEPS, turned[:EDGE], turned[width - EDGE :])
 
         tile_out[a] = tile_f[...].reshape(chunks, rows * EDGE, LANES).astype(BF16)
-        for s in range(2):
-            only(1 - 2 * s, lambda: band_copy(a, s).start())
         for k in range(len(SIDES)):
             only(-SIDES[k][0], lambda: tile_copy(a, k).start())
-        if a == 1:
-            send_round(0, 1)
 
     for k in range(1, n_lat):
         for h in range(len(parts)):
             send_round(k, h)
 
+    small_loads[0].wait()
     matrix = jac_in[...].astype(F32)
     matrix = jnp.concatenate([matrix, jnp.zeros((height - comps, planes), F32)], axis=0)
     if chunks * LANES > planes:
         matrix = jnp.concatenate([matrix, jnp.zeros((height, chunks * LANES - planes), F32)], axis=1)
     jac[...] = matrix.astype(BF16)
-    scale[...] = jnp.broadcast_to(to_column(weight_in[...], height), scale.shape)
+    scale[...] = jnp.broadcast_to(to_column(weight_in[...].reshape(1, comps), height), scale.shape)
 
     def pad_line(h):
         return comps - parts[h][0]
@@ -395,9 +411,13 @@
 
             def arrived():
                 band_copy(a, s).wait_recv()
-                for r in range(STEPS):
+                band_f[0 : area // 2, :] = band_in[a, s].astype(F32)
+
+                @pl.loop(0, STEPS)
+                def _(r):
                     for j in range(chunks):
-                        grid[j, first + r, EDGE : EDGE + width, :] = band_in[a, s, r, j].astype(F32)
+                        piece = band_f[pl.ds(j * STEPS * LANES + r, LANES, stride=STEPS), :]
+                        grid[j, first + r, EDGE : EDGE + width, :] = jnp.transpose(piece)
 
             def closed():
                 for r in range(STEPS):
@@ -440,9 +460,11 @@
                 field[j, r] = here + (down - above) + (along - pltpu.roll(along, 1, 0))
                 return below, down
 
-            lax.fori_loop(first, last, line, (here, above))
+            lax.fori_loop(first, last, line, (here, above), unroll=2)
 
     def make_state():
+        if chunks * LANES > planes:
+            band_f[area // 2 :, :] = jnp.zeros((chunks * LANES * STEPS - area // 2, width), F32)
         fill_edges(1, coef)
 
         @pl.loop(0, chunks)
@@ -618,16 +640,17 @@
             pltpu.VMEM(source.shape, BF16),
             pltpu.VMEM((TAIL * blocks, soundings), BF16),
         ]
+    small = (jnp.transpose(jacobian), obs_weight, owner.reshape(1, blocks), counts[None, :], columns)
     n_parts, n_sides = len(parts), len(SIDES)
     grid = pltpu.VMEM((chunks, extent, wide, LANES), F32)
     dma = pltpu.SemaphoreType.DMA
     result = pl.pallas_call(
         functools.partial(main_kernel, n_lat, n_lon, planes, parts, packed),
         out_shape=jax.ShapeDtypeStruct((planes * rows, width), F32),
-        in_specs=[pl.BlockSpec(memory_space=pl.ANY)] * 3
-        + [pl.BlockSpec(memory_space=pltpu.VMEM)] * 5,
+        in_specs=[pl.BlockSpec(memory_space=pl.ANY)] * (3 + len(small)),
         out_specs=pl.BlockSpec(memory_space=pl.ANY),
-        scratch_shapes=extra
+        scratch_shapes=[pltpu.VMEM(x.shape, x.dtype) for x in small]
+        + extra
         + [
             pltpu.VMEM(slots_shape, BF16),
             pltpu.VMEM((2, height, cells), F32),
@@ -640,8 +663,9 @@
             pltpu.VMEM((height, LANES), F32),
             grid, grid, grid,
             pltpu.VMEM((2, chunks * LANES * rows, width), F32),
-            pltpu.VMEM((2, rows, chunks, width, LANES), BF16),
-            pltpu.VMEM((2, 2, STEPS, chunks, width, LANES), BF16),
+            pltpu.VMEM((2, 2, planes * STEPS, width), BF16),
+            pltpu.VMEM((2, 2, planes * STEPS, width), BF16),
+            pltpu.VMEM((chunks * LANES * STEPS, width), F32),
             pltpu.VMEM((chunks, rows, EDGE, LANES), F32),
             pltpu.VMEM((2, chunks, rows * EDGE, LANES), BF16),
             pltpu.VMEM((2, n_sides, chunks, rows * EDGE, LANES), BF16),
@@ -650,7 +674,7 @@
             pltpu.VMEM((height, STEPS * width), BF16),
             pltpu.VMEM((rows * EDGE, height), BF16),
             pltpu.VMEM((n_sides, rows * EDGE, height), BF16),
-            dma((3,)), dma((n_lat, n_parts)),
+            dma((3 + len(small),)), dma((n_lat, n_parts)),
             dma((n_lat, n_parts, n_lon)), dma((n_lat, n_parts, n_lon)),
             dma((n_lat, n_parts)), dma((n_lat + 1, n_parts)),
             dma((2, 2)), dma((2, 2)), dma((2, n_sides)), dma((2, n_sides)),
@@ -662,7 +686,7 @@
         ),
     )(
         source, control.reshape(planes * rows, width), kappa.reshape(planes * rows, width),
-        jnp.transpose(jacobian), obs_weight[None, :], owner.reshape(1, blocks), counts[None, :], columns,
+        *small,
     )
     return result.reshape(control.shape)
 

time: 94.5 us -> 93.5 us (0.989); the launches traced: 94.3 us -> 91.8 us
  local copies, waits for them, and re-layouts: 3.82 us -> 2.58 us
  Pallas kernels: 90.4 us -> 89.2 us
    broadcast_in_dim x1 -> x0, local copies, waits for them, and re-layouts: 1.24 us -> none  [per_device(): obs_weight[None, :]]
    pallas_call x1, Pallas kernels: 90.4 us -> 89.2 us  [per_device(): pl.pallas_call(functools.partial(main_kernel, n_lat, n_lon, planes, parts...]
where the time goes in v3:
time: 93.5 us; the launch traced here: 91.8 us
  Pallas kernels  89.2 us (95%)
  local copies, waits for them, and re-layouts  2.58 us (3%)
    pallas_call x1, Pallas kernels, per_device(): pl.pallas_call(functools.partial(main_kernel, n_lat, n_lon, planes, parts...  89.2 us
    unnamed x1, local copies, waits for them, and re-layouts  2.58 us

profile of v3, /device:TPU:1, one launch (start us, length us, event | category | flops | bytes accessed | tf_op | source)
XLA Modules:
  0.0 91.8 jit_solution(12241060167279131991)
XLA Ops:
  0.0 89.2 %shard_map.82 = f32[2880,128]{1,0:T(8,128)} custom-call(bf16[9600,128]{1,0:T(8,128)(2,1)} %bitcast.10, f32[2880,128]{1,0:T(8,128)} %bitcast.11, f32[2880,128]{1,0:T(8,128)} %bitcast.12, bf16[300,360]{1,0:T(8,128)(2,1)} %bitcast.13, f32[300]{0:T(512)} %refs_4_.1, s32[1,32]{1,0:T(1,128)} %bitcast.14, s32[1,32]{1,0:T(1,128)} %bitcast.15, s32[32,128]{1,0:T(8,128)} %refs_7_.1), custom_call_target="tpu_custom_call" | custom-call | tf_op jit(solution)/shard_map/pallas_call | solution.py:647
  89.2 2.6 %copy.10 = f32[4,90,8,128]{3,2,1,0:T(8,128)} copy(f32[4,90,8,128]{3,2,1,0:T(8,128)} %bitcast.9) | data formatting | bytes 2949120

commit v4 on v3

--- a/solution.py
+++ b/solution.py
@@ -114,7 +114,6 @@
     area = planes * rows
     step_rows = LANES * rows
     slots = n_lon * CAP
-    band_rows = STEPS * EDGE
 
     def plane_of(k):
         mirrored = lat >= n_lat - n_lat // 2
@@ -178,18 +177,8 @@
     def peer(k):
         return (lat - SIDES[k][0], around(-SIDES[k][1]))
 
-    def side_span(k):
-        step = SIDES[k][0]
-        if step == 0:
-            return pl.ds(0, rows * EDGE)
-        return pl.ds((rows * EDGE - band_rows) if step < 0 else 0, band_rows)
-
     def tile_copy(a, k):
-        span = side_span(k)
-        return remote(
-            tile_out.at[a, :, span, :], tile_in.at[a, k, :, span, :],
-            tile_send.at[a, k], tile_recv.at[a, k], peer(k),
-        )
+        return remote(tile_out.at[a, 1 - k], tile_in.at[a, k], tile_send.at[a, k], tile_recv.at[a, k], peer(k))
 
     def row_copy(h, s):
         lo, size = parts[h]
@@ -201,9 +190,11 @@
         )
 
     def side_copy(k):
-        span = side_span(k)
+        step, side = SIDES[k]
+        span = pl.ds((rows - STEPS) * STEPS if step < 0 else 0, (STEPS if step else rows) * STEPS)
         return remote(
-            side_out.at[span, :], side_in.at[k, span, :], side_send.at[k], side_recv.at[k], peer(k)
+            side_out.at[(1 - side) // 2, span, :], side_in.at[k, span, :],
+            side_send.at[k], side_recv.at[k], peer(k),
         )
 
     loads = [
@@ -319,11 +310,6 @@
             for j in range(chunks):
                 turned = jnp.transpose(raw[a, pl.ds(j * step_rows + r, LANES, stride=rows), :])
                 grid[j, STEPS + r, EDGE : EDGE + width, :] = turned
-                tile_f[j, r] = jnp.where(sub < STEPS, turned[:EDGE], turned[width - EDGE :])
-
-        tile_out[a] = tile_f[...].reshape(chunks, rows * EDGE, LANES).astype(BF16)
-        for k in range(len(SIDES)):
-            only(-SIDES[k][0], lambda: tile_copy(a, k).start())
 
     for k in range(1, n_lat):
         for h in range(len(parts)):
@@ -401,11 +387,10 @@
 
         part_sent(k, h).start()
 
-    def join(k):
-        for h in range(len(parts)):
-            pl.when(has(-1) & has(1))(lambda: emit(k, h, True))
-
-    def fill_edges(a, grid):
+    def join(k, h):
+        pl.when(has(-1) & has(1))(lambda: emit(k, h, True))
+
+    def fill_rows(a, grid):
         def band(s):
             first = (rows + STEPS) * s
 
@@ -430,21 +415,36 @@
         for s in range(2):
             band(s)
 
-        def sides(west, count, place, source_row):
-            tile_copy(a, west).wait_recv()
-            tile_copy(a, west + 1).wait_recv()
-            span = slice(source_row * EDGE, (source_row + count) * EDGE)
-            shape = (chunks, count, EDGE, LANES)
-            both = [tile_in[a, k, :, span, :].astype(F32).reshape(shape) for k in (west, west + 1)]
+        @pl.loop(0, extent // 2)
+        def _(p):
             for j in range(chunks):
-                for r in range(count):
-                    tile = jnp.where(sub < STEPS, both[1][j, r], both[0][j, r])
-                    grid[j, place + r, 0:EDGE, :] = tile
-                    grid[j, place + r, EDGE + width :, :] = tile
-
-        sides(0, rows, STEPS, 0)
-        only(-1, lambda: sides(2, STEPS, 0, rows - STEPS))
-        only(1, lambda: sides(4, STEPS, rows + STEPS, 0))
+                left = [grid[j, 2 * p + q, EDGE : 2 * EDGE, :] for q in range(2)]
+                right = [grid[j, 2 * p + q, width : width + EDGE, :] for q in range(2)]
+                tile_f[0, j, p] = jnp.where(sub < STEPS, left[0], pltpu.roll(left[1], STEPS, 0))
+                tile_f[1, j, p] = jnp.where(sub < STEPS, pltpu.roll(right[0], STEPS, 0), right[1])
+
+        tile_out[a] = tile_f[...].reshape(2, chunks, extent * STEPS, LANES).astype(BF16)
+        for k in range(2):
+            tile_copy(a, k).start()
+
+    def put_sides(grid, j, p, west, east_):
+        pair = (
+            jnp.where(sub < STEPS, east_, pltpu.roll(west, STEPS, 0)),
+            jnp.where(sub < STEPS, pltpu.roll(east_, STEPS, 0), west),
+        )
+        for q in range(2):
+            grid[j, 2 * p + q, 0:EDGE, :] = pair[q]
+            grid[j, 2 * p + q, EDGE + width :, :] = pair[q]
+
+    def fill_columns(a, grid):
+        for k in range(2):
+            tile_copy(a, k).wait_recv()
+        west, east_ = (
+            tile_in[a, k].astype(F32).reshape(chunks, extent // 2, EDGE, LANES) for k in range(2)
+        )
+        for j in range(chunks):
+            for p in range(extent // 2):
+                put_sides(grid, j, p, west[j, p], east_[j, p])
 
     def spread(j):
         for step in range(STEPS):
@@ -462,10 +462,16 @@
 
             lax.fori_loop(first, last, line, (here, above), unroll=2)
 
-    def make_state():
+    def take_kappa():
         if chunks * LANES > planes:
             band_f[area // 2 :, :] = jnp.zeros((chunks * LANES * STEPS - area // 2, width), F32)
-        fill_edges(1, coef)
+        fill_rows(1, coef)
+
+    def take_control():
+        fill_rows(0, field)
+
+    def make_state():
+        fill_columns(1, coef)
 
         @pl.loop(0, chunks)
         def _(j):
@@ -475,9 +481,10 @@
                 east[j, r] = here * pltpu.roll(here, wide - 1, 0)
                 coef[j, r] = here * coef[j, r + 1]
 
-        fill_edges(0, field)
+        fill_columns(0, field)
         pl.loop(0, chunks)(spread)
 
+    def make_model():
         @pl.loop(0, rows)
         def _(r):
             state = jnp.concatenate(
@@ -487,14 +494,18 @@
                 jac[...], state, (((1,), (1,)), ((), ())), preferred_element_type=F32
             )
 
+    stages = [take_kappa, take_control, make_state, make_model]
     for k in range(n_lat - 1):
         for h in range(len(parts)):
             reduce(k, h)
-        if k > 0:
-            join(k - 1)
-        if k == min(1, n_lat - 2):
-            make_state()
-    join(n_lat - 2)
+            if k > 0:
+                join(k - 1, h)
+            if k == n_lat - 2:
+                join(k, h)
+            if stages and k * len(parts) + h > 0:
+                stages.pop(0)()
+    for stage in stages:
+        stage()
     for h in range(len(parts)):
         reduce(n_lat - 1, h)
 
@@ -529,14 +540,15 @@
         for s in range(2):
             only(1 - 2 * s, lambda: row_copy(h, s).start())
 
-    ends = (rows * EDGE, cells)
+    ends = (2 * rows * STEPS, cells)
     line = iota(ends, 0)
-    spot = jnp.bitwise_and(line, EDGE - 1)
-    spot = (line // EDGE) * width + jnp.where(spot < STEPS, spot, spot + width - EDGE)
+    spot = lax.rem(line, rows * STEPS)
+    spot = (spot // STEPS) * width + lax.rem(spot, STEPS)
+    spot = spot + jnp.where(line < rows * STEPS, 0, width - STEPS)
     ends = jnp.where(iota(ends, 1) == spot, 1.0, 0.0).astype(BF16)
     side_out[...] = lax.dot_general(
         ends, total[...], (((1,), (1,)), ((), ())), preferred_element_type=F32
-    ).astype(BF16)
+    ).reshape(2, rows * STEPS, height).astype(BF16)
     for k in range(len(SIDES)):
         only(-SIDES[k][0], lambda: side_copy(k).start())
 
@@ -552,25 +564,22 @@
     for k in range(len(SIDES)):
         only(SIDES[k][0], lambda: side_copy(k).wait_recv())
 
-    def west_east(west, span):
-        values = [side_in[k, span, :].astype(F32) for k in (west, west + 1)]
-        left = jnp.bitwise_and(iota(values[0].shape, 0), EDGE - 1) < STEPS
-        return jnp.where(left, values[1], values[0])
-
     side = jnp.concatenate(
         [
-            west_east(2, slice((rows - STEPS) * EDGE, rows * EDGE)),
-            west_east(0, slice(0, rows * EDGE)),
-            west_east(4, slice(0, band_rows)),
+            side_in[k, lines, :]
+            for ks in ((2, 0, 4), (3, 1, 5))
+            for k, lines in zip(ks, (slice((rows - STEPS) * STEPS, rows * STEPS), slice(None), slice(0, STEPS * STEPS)))
         ],
         axis=0,
-    ).astype(BF16)
+    )
     result = jnp.dot(side, jac[...], preferred_element_type=F32)
     for j in range(chunks):
-        for r in range(extent):
-            piece = result[r * EDGE : (r + 1) * EDGE, j * LANES : (j + 1) * LANES]
-            field[j, r, 0:EDGE, :] = piece
-            field[j, r, EDGE + width :, :] = piece
+        for p in range(extent // 2):
+            west, east_ = (
+                result[first + p * EDGE : first + (p + 1) * EDGE, j * LANES : (j + 1) * LANES]
+                for first in (0, extent * STEPS)
+            )
+            put_sides(field, j, p, west, east_)
 
     for h in range(len(parts)):
         for s in range(2):
@@ -610,8 +619,8 @@
     for a in range(2):
         for s in range(2):
             only(1 - 2 * s, lambda: band_copy(a, s).wait_send())
-        for k in range(len(SIDES)):
-            only(-SIDES[k][0], lambda: tile_copy(a, k).wait_send())
+        for k in range(2):
+            tile_copy(a, k).wait_send()
     for store in stores:
         store.wait()
 
@@ -666,18 +675,18 @@
             pltpu.VMEM((2, 2, planes * STEPS, width), BF16),
             pltpu.VMEM((2, 2, planes * STEPS, width), BF16),
             pltpu.VMEM((chunks * LANES * STEPS, width), F32),
-            pltpu.VMEM((chunks, rows, EDGE, LANES), F32),
-            pltpu.VMEM((2, chunks, rows * EDGE, LANES), BF16),
-            pltpu.VMEM((2, n_sides, chunks, rows * EDGE, LANES), BF16),
+            pltpu.VMEM((2, chunks, extent // 2, EDGE, LANES), F32),
+            pltpu.VMEM((2, 2, chunks, extent * STEPS, LANES), BF16),
+            pltpu.VMEM((2, 2, chunks, extent * STEPS, LANES), BF16),
             pltpu.VMEM((height, cells), BF16),
             pltpu.VMEM((height, STEPS * width), BF16),
             pltpu.VMEM((height, STEPS * width), BF16),
-            pltpu.VMEM((rows * EDGE, height), BF16),
-            pltpu.VMEM((n_sides, rows * EDGE, height), BF16),
+            pltpu.VMEM((2, rows * STEPS, height), BF16),
+            pltpu.VMEM((n_sides, rows * STEPS, height), BF16),
             dma((3 + len(small),)), dma((n_lat, n_parts)),
             dma((n_lat, n_parts, n_lon)), dma((n_lat, n_parts, n_lon)),
             dma((n_lat, n_parts)), dma((n_lat + 1, n_parts)),
-            dma((2, 2)), dma((2, 2)), dma((2, n_sides)), dma((2, n_sides)),
+            dma((2, 2)), dma((2, 2)), dma((2, 2)), dma((2, 2)),
             dma((n_parts, 2)), dma((n_parts, 2)), dma((n_sides,)), dma((n_sides,)),
             dma((chunks,)),
         ],

time: 93.5 us -> 108 us (1.16)
  Pallas kernels: 89.2 us -> 104 us
    pallas_call x1, Pallas kernels: 89.2 us -> 104 us  [per_device(): pl.pallas_call(functools.partial(main_kernel, n_lat, n_lon, planes, parts...]
where the time goes in v4:
time: 108 us; the launch traced here: 107 us
  Pallas kernels  104 us (96%)
  local copies, waits for them, and re-layouts  2.58 us (2%)
    pallas_call x1, Pallas kernels, per_device(): pl.pallas_call(functools.partial(main_kernel, n_lat, n_lon, planes, parts...  104 us
    unnamed x1, local copies, waits for them, and re-layouts  2.58 us

profile of v4, /device:TPU:1, one launch (start us, length us, event | category | flops | bytes accessed | tf_op | source)
XLA Modules:
  0.0 107.1 jit_solution(7192684464219675548)
XLA Ops:
  0.0 104.5 %shard_map.82 = f32[2880,128]{1,0:T(8,128)} custom-call(bf16[9600,128]{1,0:T(8,128)(2,1)} %bitcast.10, f32[2880,128]{1,0:T(8,128)} %bitcast.11, f32[2880,128]{1,0:T(8,128)} %bitcast.12, bf16[300,360]{1,0:T(8,128)(2,1)} %bitcast.13, f32[300]{0:T(512)} %refs_4_.1, s32[1,32]{1,0:T(1,128)} %bitcast.14, s32[1,32]{1,0:T(1,128)} %bitcast.15, s32[32,128]{1,0:T(8,128)} %refs_7_.1), custom_call_target="tpu_custom_call" | custom-call | tf_op jit(solution)/shard_map/pallas_call | solution.py:656
  104.5 2.6 %copy.10 = f32[4,90,8,128]{3,2,1,0:T(8,128)} copy(f32[4,90,8,128]{3,2,1,0:T(8,128)} %bitcast.9) | data formatting | bytes 2949120

commit v5 on v4

--- a/solution.py
+++ b/solution.py
@@ -177,8 +177,19 @@
     def peer(k):
         return (lat - SIDES[k][0], around(-SIDES[k][1]))
 
+    def side_span(k):
+        step = SIDES[k][0]
+        return pl.ds((rows - STEPS) * STEPS if step < 0 else 0, (STEPS if step else rows) * STEPS)
+
+    def side_of(k):
+        return (1 - SIDES[k][1]) // 2
+
     def tile_copy(a, k):
-        return remote(tile_out.at[a, 1 - k], tile_in.at[a, k], tile_send.at[a, k], tile_recv.at[a, k], peer(k))
+        span = side_span(k)
+        return remote(
+            tile_out.at[a, side_of(k), :, span, :], tile_in.at[a, k, :, span, :],
+            tile_send.at[a, k], tile_recv.at[a, k], peer(k),
+        )
 
     def row_copy(h, s):
         lo, size = parts[h]
@@ -190,11 +201,9 @@
         )
 
     def side_copy(k):
-        step, side = SIDES[k]
-        span = pl.ds((rows - STEPS) * STEPS if step < 0 else 0, (STEPS if step else rows) * STEPS)
+        span = side_span(k)
         return remote(
-            side_out.at[(1 - side) // 2, span, :], side_in.at[k, span, :],
-            side_send.at[k], side_recv.at[k], peer(k),
+            side_out.at[side_of(k), span, :], side_in.at[k, span, :], side_send.at[k], side_recv.at[k], peer(k)
         )
 
     loads = [
@@ -311,6 +320,19 @@
                 turned = jnp.transpose(raw[a, pl.ds(j * step_rows + r, LANES, stride=rows), :])
                 grid[j, STEPS + r, EDGE : EDGE + width, :] = turned
 
+        @pl.loop(0, rows // 2)
+        def _(p):
+            for j in range(chunks):
+                pair = [STEPS + 2 * p + q for q in range(2)]
+                left = [grid[j, r, EDGE : 2 * EDGE, :] for r in pair]
+                right = [grid[j, r, width : width + EDGE, :] for r in pair]
+                tile_f[0, j, p] = jnp.where(sub < STEPS, left[0], pltpu.roll(left[1], STEPS, 0))
+                tile_f[1, j, p] = jnp.where(sub < STEPS, pltpu.roll(right[0], STEPS, 0), right[1])
+
+        tile_out[a] = tile_f[...].reshape(2, chunks, rows * STEPS, LANES).astype(BF16)
+        for k in range(len(SIDES)):
+            only(-SIDES[k][0], lambda: tile_copy(a, k).start())
+
     for k in range(1, n_lat):
         for h in range(len(parts)):
             send_round(k, h)
@@ -415,18 +437,6 @@
         for s in range(2):
             band(s)
 
-        @pl.loop(0, extent // 2)
-        def _(p):
-            for j in range(chunks):
-                left = [grid[j, 2 * p + q, EDGE : 2 * EDGE, :] for q in range(2)]
-                right = [grid[j, 2 * p + q, width : width + EDGE, :] for q in range(2)]
-                tile_f[0, j, p] = jnp.where(sub < STEPS, left[0], pltpu.roll(left[1], STEPS, 0))
-                tile_f[1, j, p] = jnp.where(sub < STEPS, pltpu.roll(right[0], STEPS, 0), right[1])
-
-        tile_out[a] = tile_f[...].reshape(2, chunks, extent * STEPS, LANES).astype(BF16)
-        for k in range(2):
-            tile_copy(a, k).start()
-
     def put_sides(grid, j, p, west, east_):
         pair = (
             jnp.where(sub < STEPS, east_, pltpu.roll(west, STEPS, 0)),
@@ -437,14 +447,21 @@
             grid[j, 2 * p + q, EDGE + width :, :] = pair[q]
 
     def fill_columns(a, grid):
-        for k in range(2):
-            tile_copy(a, k).wait_recv()
-        west, east_ = (
-            tile_in[a, k].astype(F32).reshape(chunks, extent // 2, EDGE, LANES) for k in range(2)
-        )
-        for j in range(chunks):
-            for p in range(extent // 2):
-                put_sides(grid, j, p, west[j, p], east_[j, p])
+        def sides(k, place, source_row, count):
+            for side in (k, k + 1):
+                tile_copy(a, side).wait_recv()
+            span = slice(source_row * STEPS, (source_row + count) * STEPS)
+            west, east_ = (
+                tile_in[a, side, :, span, :].astype(F32).reshape(chunks, count // 2, EDGE, LANES)
+                for side in (k, k + 1)
+            )
+            for j in range(chunks):
+                for p in range(count // 2):
+                    put_sides(grid, j, place // 2 + p, west[j, p], east_[j, p])
+
+        sides(0, STEPS, 0, rows)
+        only(-1, lambda: sides(2, 0, rows - STEPS, STEPS))
+        only(1, lambda: sides(4, STEPS + rows, 0, STEPS))
 
     def spread(j):
         for step in range(STEPS):
@@ -619,8 +636,8 @@
     for a in range(2):
         for s in range(2):
             only(1 - 2 * s, lambda: band_copy(a, s).wait_send())
-        for k in range(2):
-            tile_copy(a, k).wait_send()
+        for k in range(len(SIDES)):
+            only(-SIDES[k][0], lambda: tile_copy(a, k).wait_send())
     for store in stores:
         store.wait()
 
@@ -675,9 +692,9 @@
             pltpu.VMEM((2, 2, planes * STEPS, width), BF16),
             pltpu.VMEM((2, 2, planes * STEPS, width), BF16),
             pltpu.VMEM((chunks * LANES * STEPS, width), F32),
-            pltpu.VMEM((2, chunks, extent // 2, EDGE, LANES), F32),
-            pltpu.VMEM((2, 2, chunks, extent * STEPS, LANES), BF16),
-            pltpu.VMEM((2, 2, chunks, extent * STEPS, LANES), BF16),
+            pltpu.VMEM((2, chunks, rows // 2, EDGE, LANES), F32),
+            pltpu.VMEM((2, 2, chunks, rows * STEPS, LANES), BF16),
+            pltpu.VMEM((2, n_sides, chunks, rows * STEPS, LANES), BF16),
             pltpu.VMEM((height, cells), BF16),
             pltpu.VMEM((height, STEPS * width), BF16),
             pltpu.VMEM((height, STEPS * width), BF16),
@@ -686,7 +703,7 @@
             dma((3 + len(small),)), dma((n_lat, n_parts)),
             dma((n_lat, n_parts, n_lon)), dma((n_lat, n_parts, n_lon)),
             dma((n_lat, n_parts)), dma((n_lat + 1, n_parts)),
-            dma((2, 2)), dma((2, 2)), dma((2, 2)), dma((2, 2)),
+            dma((2, 2)), dma((2, 2)), dma((2, n_sides)), dma((2, n_sides)),
             dma((n_parts, 2)), dma((n_parts, 2)), dma((n_sides,)), dma((n_sides,)),
             dma((chunks,)),
         ],

time: 108 us -> 90.2 us (0.84)
  Pallas kernels: 104 us -> 86 us
    pallas_call x1, Pallas kernels: 104 us -> 86 us  [per_device(): pl.pallas_call(functools.partial(main_kernel, n_lat, n_lon, planes, parts...]
where the time goes in v5:
time: 90.2 us; the launch traced here: 88.6 us
  Pallas kernels  86 us (95%)
  local copies, waits for them, and re-layouts  2.58 us (3%)
    pallas_call x1, Pallas kernels, per_device(): pl.pallas_call(functools.partial(main_kernel, n_lat, n_lon, planes, parts...  86 us
    unnamed x1, local copies, waits for them, and re-layouts  2.58 us

profile of v5, /device:TPU:1, one launch (start us, length us, event | category | flops | bytes accessed | tf_op | source)
XLA Modules:
  0.0 88.6 jit_solution(12438723694492017907)
XLA Ops:
  0.0 86.0 %shard_map.82 = f32[2880,128]{1,0:T(8,128)} custom-call(bf16[9600,128]{1,0:T(8,128)(2,1)} %bitcast.10, f32[2880,128]{1,0:T(8,128)} %bitcast.11, f32[2880,128]{1,0:T(8,128)} %bitcast.12, bf16[300,360]{1,0:T(8,128)(2,1)} %bitcast.13, f32[300]{0:T(512)} %refs_4_.1, s32[1,32]{1,0:T(1,128)} %bitcast.14, s32[1,32]{1,0:T(1,128)} %bitcast.15, s32[32,128]{1,0:T(8,128)} %refs_7_.1), custom_call_target="tpu_custom_call" | custom-call | tf_op jit(solution)/shard_map/pallas_call | solution.py:673
  86.1 2.6 %copy.10 = f32[4,90,8,128]{3,2,1,0:T(8,128)} copy(f32[4,90,8,128]{3,2,1,0:T(8,128)} %bitcast.9) | data formatting | bytes 2949120

commit v6 on v5

--- a/solution.py
+++ b/solution.py
@@ -214,12 +214,12 @@
         pltpu.make_async_copy(ref, to, load_sem.at[3 + n]) for n, (ref, to) in enumerate(zip(small_in, small))
     ]
     loads[1].start()
-    loads[0].start()
     for load in small_loads[1:]:
         load.start()
     if not packed:
         obs_load = pltpu.make_async_copy(source, obs, load_sem.at[2])
         obs_load.start()
+    loads[0].start()
     small_loads[0].start()
 
     barrier = pltpu.get_barrier_semaphore()
@@ -238,7 +238,8 @@
         only(step, greet)
 
     sub = iota((EDGE, LANES), 0)
-    for a in (1, 0):
+
+    def send_bands(a):
         loads[a].wait()
         if chunks * step_rows > area:
             raw[a, area:, :] = jnp.zeros((chunks * step_rows - area, width), F32)
@@ -254,6 +255,7 @@
         for s in range(2):
             only(1 - 2 * s, lambda: band_copy(a, s).start())
 
+    send_bands(1)
     for load in small_loads[1:]:
         load.wait()
 
@@ -312,6 +314,8 @@
         obs_load.wait()
     for h in range(len(parts)):
         send_round(0, h)
+        if h == 0:
+            send_bands(0)
 
     for a, grid in ((1, coef), (0, field)):
         @pl.loop(0, rows)
@@ -351,17 +355,16 @@
     def lanes(n):
         return pl.ds(pl.multiple_of(n * TILE, TILE), TILE)
 
-    def reduce(k, h):
+    def reduce_peers(k, h, start, stop):
         lo, size = parts[h]
 
-        @pl.loop(1, n_lon)
+        @pl.loop(max(start, 1), stop)
         def _(i):
             block_copy(k, h, i).wait_recv()
 
-        own_copy(k, h).wait()
         base = height - GROUP
         first = comps - base
-        heads = [recv[k, i, c, base:height, :].astype(F32) for i in range(n_lon) for c in range(CAP)]
+        heads = [recv[k, i, c, base:height, :].astype(F32) for i in range(start, stop) for c in range(CAP)]
         code = jnp.concatenate(
             [(x[first + 1 : first + 2] - 1.0) * 32.0 + x[first + 2 : first + 3] for x in heads], axis=1
         ).astype(jnp.int32)
@@ -369,18 +372,23 @@
         @pl.loop(0, cells // TILE)
         def _(n):
             values = jnp.concatenate(
-                [recv[k, i, c, lo : lo + size, :] for i in range(n_lon) for c in range(CAP)], axis=1
+                [recv[k, i, c, lo : lo + size, :] for i in range(start, stop) for c in range(CAP)], axis=1
             )
             hot = jnp.where(iota((TILE, code.shape[1]), 0) == code - n * TILE, 1.0, 0.0).astype(BF16)
             part = lax.dot_general(values, hot, (((1,), (1,)), ((), ())), preferred_element_type=F32)
-            if k == n_lat - 1:
-                sums[lo : lo + size, lanes(n)] = part
-                if h == 0:
-                    line = pad_line(h)
-                    number[:, lanes(n)] = jnp.broadcast_to(part[line : line + 1], (8, TILE))
-            else:
-                ring[k % 2, lo : lo + size, lanes(n)] = part
-
+            target = sums.at[lo : lo + size, lanes(n)]
+            if k < n_lat - 1:
+                target = ring.at[k % 2, lo : lo + size, lanes(n)]
+            target[...] = part if start == 0 else target[...] + part
+            if k == n_lat - 1 and h == 0:
+                line = pad_line(h)
+                number[:, lanes(n)] = jnp.broadcast_to(part[line : line + 1], (8, TILE))
+
+    def reduce(k, h, groups=1):
+        own_copy(k, h).wait()
+        for g in range(groups):
+            peers = n_lon // groups
+            reduce_peers(k, h, g * peers, (g + 1) * peers)
         if k < n_lat - 1:
             pl.when(jnp.logical_not(has(-1) & has(1)))(lambda: emit(k, h, False))
 
@@ -466,18 +474,16 @@
     def spread(j):
         for step in range(STEPS):
             first, last = step + 1, extent - 1 - step
-            here = field[j, first]
-            above = coef[j, first - 1] * (here - field[j, first - 1])
-
-            def line(r, carry):
-                here, above = carry
-                below = field[j, r + 1]
-                down = coef[j, r] * (below - here)
+            above = coef[j, first - 1] * (field[j, first] - field[j, first - 1])
+
+            def line(r, above):
+                here = field[j, r]
+                down = coef[j, r] * (field[j, r + 1] - here)
                 along = east[j, r] * (pltpu.roll(here, wide - 1, 0) - here)
                 field[j, r] = here + (down - above) + (along - pltpu.roll(along, 1, 0))
-                return below, down
-
-            lax.fori_loop(first, last, line, (here, above), unroll=2)
+                return down
+
+            lax.fori_loop(first, last, line, above, unroll=2)
 
     def take_kappa():
         if chunks * LANES > planes:
@@ -523,8 +529,6 @@
                 stages.pop(0)()
     for stage in stages:
         stage()
-    for h in range(len(parts)):
-        reduce(n_lat - 1, h)
 
     for s, ref in enumerate((total_north, total_south)):
         def blank():
@@ -548,6 +552,7 @@
                 number[:, lanes(n)] = number[:, lanes(n)] + count
 
     for h, (lo, size) in enumerate(parts):
+        reduce(n_lat - 1, h, groups=2 if h == len(parts) - 1 else 1)
         only(-1, lambda: add_part(lat, h))
         only(1, lambda: add_part(n_lat, h))
         for r in range(rows):
@@ -651,7 +656,7 @@
     height = comps + TAIL
     chunks = -(-planes // LANES)
     extent, wide = rows + 2 * STEPS, width + 2 * EDGE
-    half = -(-height // 64) * 32
+    half = height // 96 * 32
     parts = ((half, height - half), (0, half))
     obs = jnp.transpose(pc_obs, (2, 0, 1))
     slots_shape = (n_lat, n_lon, CAP, height, soundings)

time: 90.2 us -> 86 us (0.953)
  Pallas kernels: 86 us -> 81.7 us
    pallas_call x1, Pallas kernels: 86 us -> 81.7 us  [per_device(): pl.pallas_call(functools.partial(main_kernel, n_lat, n_lon, planes, parts...]
where the time goes in v6:
time: 86 us; the launch traced here: 84.3 us
  Pallas kernels  81.7 us (95%)
  local copies, waits for them, and re-layouts  2.58 us (3%)
    pallas_call x1, Pallas kernels, per_device(): pl.pallas_call(functools.partial(main_kernel, n_lat, n_lon, planes, parts...  81.7 us
    unnamed x1, local copies, waits for them, and re-layouts  2.58 us

profile of v6, /device:TPU:1, one launch (start us, length us, event | category | flops | bytes accessed | tf_op | source)
XLA Modules:
  0.0 84.3 jit_solution(15571441074759842992)
XLA Ops:
  0.0 81.7 %shard_map.82 = f32[2880,128]{1,0:T(8,128)} custom-call(bf16[9600,128]{1,0:T(8,128)(2,1)} %bitcast.10, f32[2880,128]{1,0:T(8,128)} %bitcast.11, f32[2880,128]{1,0:T(8,128)} %bitcast.12, bf16[300,360]{1,0:T(8,128)(2,1)} %bitcast.13, f32[300]{0:T(512)} %refs_4_.1, s32[1,32]{1,0:T(1,128)} %bitcast.14, s32[1,32]{1,0:T(1,128)} %bitcast.15, s32[32,128]{1,0:T(8,128)} %refs_7_.1), custom_call_target="tpu_custom_call" | custom-call | tf_op jit(solution)/shard_map/pallas_call | solution.py:678
  81.7 2.6 %copy.10 = f32[4,90,8,128]{3,2,1,0:T(8,128)} copy(f32[4,90,8,128]{3,2,1,0:T(8,128)} %bitcast.9) | data formatting | bytes 2949120

commit v7 on v6

--- a/solution.py
+++ b/solution.py
@@ -471,7 +471,7 @@
         only(-1, lambda: sides(2, 0, rows - STEPS, STEPS))
         only(1, lambda: sides(4, STEPS + rows, 0, STEPS))
 
-    def spread(j):
+    def spread(j, finish=None):
         for step in range(STEPS):
             first, last = step + 1, extent - 1 - step
             above = coef[j, first - 1] * (field[j, first] - field[j, first - 1])
@@ -480,7 +480,11 @@
                 here = field[j, r]
                 down = coef[j, r] * (field[j, r + 1] - here)
                 along = east[j, r] * (pltpu.roll(here, wide - 1, 0) - here)
-                field[j, r] = here + (down - above) + (along - pltpu.roll(along, 1, 0))
+                result = here + (down - above) + (along - pltpu.roll(along, 1, 0))
+                if finish is not None and step == STEPS - 1:
+                    finish(r - STEPS, result[EDGE : EDGE + width])
+                else:
+                    field[j, r] = result
                 return down
 
             lax.fori_loop(first, last, line, above, unroll=2)
@@ -493,7 +497,7 @@
     def take_control():
         fill_rows(0, field)
 
-    def make_state():
+    def make_products():
         fill_columns(1, coef)
 
         @pl.loop(0, chunks)
@@ -504,6 +508,7 @@
                 east[j, r] = here * pltpu.roll(here, wide - 1, 0)
                 coef[j, r] = here * coef[j, r + 1]
 
+    def make_state():
         fill_columns(0, field)
         pl.loop(0, chunks)(spread)
 
@@ -517,7 +522,8 @@
                 jac[...], state, (((1,), (1,)), ((), ())), preferred_element_type=F32
             )
 
-    stages = [take_kappa, take_control, make_state, make_model]
+    stages = {1: [make_products, take_control], 3: [make_state, make_model]}
+    take_kappa()
     for k in range(n_lat - 1):
         for h in range(len(parts)):
             reduce(k, h)
@@ -525,10 +531,8 @@
                 join(k - 1, h)
             if k == n_lat - 2:
                 join(k, h)
-            if stages and k * len(parts) + h > 0:
-                stages.pop(0)()
-    for stage in stages:
-        stage()
+            for stage in stages.get(k * len(parts) + h, []):
+                stage()
 
     for s, ref in enumerate((total_north, total_south)):
         def blank():
@@ -615,13 +619,11 @@
 
     stores = []
     for j in range(chunks):
-        spread(j)
-
-        @pl.loop(0, rows)
-        def _(r):
+        def add_row(r, values):
             at = pl.ds(j * step_rows + r, LANES, stride=rows)
-            raw[0, at, :] = raw[0, at, :] + jnp.transpose(field[j, STEPS + r, EDGE : EDGE + width, :])
-
+            raw[0, at, :] = raw[0, at, :] + jnp.transpose(values)
+
+        spread(j, add_row)
         span = pl.ds(j * step_rows, min(step_rows, area - j * step_rows))
         stores.append(pltpu.make_async_copy(raw.at[0, span, :], out.at[span, :], store_sem.at[j]))
         stores[-1].start()

time: 86 us -> 84.4 us (0.981)
  the two profiles are of different devices: /device:TPU:1 before, /device:TPU:0 now
where the time goes in v7:
time: 84.4 us; the launch traced here: 84.3 us
  Pallas kernels  81.7 us (97%)
  local copies, waits for them, and re-layouts  2.58 us (3%)
    pallas_call x1, Pallas kernels, per_device(): pl.pallas_call(functools.partial(main_kernel, n_lat, n_lon, planes, parts...  81.7 us
    unnamed x1, local copies, waits for them, and re-layouts  2.58 us

profile of v7, /device:TPU:0, one launch (start us, length us, event | category | flops | bytes accessed | tf_op | source)
XLA Modules:
  0.0 84.3 jit_solution(4983585594588427977)
XLA Ops:
  0.0 81.7 %shard_map.82 = f32[2880,128]{1,0:T(8,128)} custom-call(bf16[9600,128]{1,0:T(8,128)(2,1)} %bitcast.10, f32[2880,128]{1,0:T(8,128)} %bitcast.11, f32[2880,128]{1,0:T(8,128)} %bitcast.12, bf16[300,360]{1,0:T(8,128)(2,1)} %bitcast.13, f32[300]{0:T(512)} %refs_4_.1, s32[1,32]{1,0:T(1,128)} %bitcast.14, s32[1,32]{1,0:T(1,128)} %bitcast.15, s32[32,128]{1,0:T(8,128)} %refs_7_.1), custom_call_target="tpu_custom_call" | custom-call | tf_op jit(solution)/shard_map/pallas_call | solution.py:680
  81.7 2.6 %copy.10 = f32[4,90,8,128]{3,2,1,0:T(8,128)} copy(f32[4,90,8,128]{3,2,1,0:T(8,128)} %bitcast.9) | data formatting | bytes 2949120

commit v8 on v7

--- a/solution.py
+++ b/solution.py
@@ -213,12 +213,12 @@
     small_loads = [
         pltpu.make_async_copy(ref, to, load_sem.at[3 + n]) for n, (ref, to) in enumerate(zip(small_in, small))
     ]
-    loads[1].start()
     for load in small_loads[1:]:
         load.start()
     if not packed:
         obs_load = pltpu.make_async_copy(source, obs, load_sem.at[2])
         obs_load.start()
+    loads[1].start()
     loads[0].start()
     small_loads[0].start()
 
@@ -248,14 +248,9 @@
         upper = iota(even.shape, 1) < STEPS
         band_out[a, 0] = jnp.where(upper, even, pltpu.roll(odd, STEPS, 1)).reshape(area // 2, width).astype(BF16)
         band_out[a, 1] = jnp.where(upper, pltpu.roll(even, STEPS, 1), odd).reshape(area // 2, width).astype(BF16)
-        if a == 1:
-            pl.semaphore_wait(
-                barrier, n_lon - 1 + 3 * (has(-1).astype(jnp.int32) + has(1).astype(jnp.int32))
-            )
         for s in range(2):
             only(1 - 2 * s, lambda: band_copy(a, s).start())
 
-    send_bands(1)
     for load in small_loads[1:]:
         load.wait()
 
@@ -303,6 +298,10 @@
     def send_round(k, h):
         if not packed:
             pack_round(k, h)
+        if k == 0 and h == 0:
+            pl.semaphore_wait(
+                barrier, n_lon - 1 + 3 * (has(-1).astype(jnp.int32) + has(1).astype(jnp.int32))
+            )
 
         @pl.loop(1, n_lon)
         def _(i):
@@ -315,6 +314,7 @@
     for h in range(len(parts)):
         send_round(0, h)
         if h == 0:
+            send_bands(1)
             send_bands(0)
 
     for a, grid in ((1, coef), (0, field)):
@@ -658,7 +658,7 @@
     height = comps + TAIL
     chunks = -(-planes // LANES)
     extent, wide = rows + 2 * STEPS, width + 2 * EDGE
-    half = height // 96 * 32
+    half = height // 64 * 32
     parts = ((half, height - half), (0, half))
     obs = jnp.transpose(pc_obs, (2, 0, 1))
     slots_shape = (n_lat, n_lon, CAP, height, soundings)

time: 84.4 us -> 83 us (0.983)
  the two profiles are of different devices: /device:TPU:0 before, /device:TPU:1 now
where the time goes in v8:
time: 83 us; the launch traced here: 81.9 us
  Pallas kernels  79.3 us (96%)
  local copies, waits for them, and re-layouts  2.58 us (3%)
    pallas_call x1, Pallas kernels, per_device(): pl.pallas_call(functools.partial(main_kernel, n_lat, n_lon, planes, parts...  79.3 us
    unnamed x1, local copies, waits for them, and re-layouts  2.58 us

profile of v8, /device:TPU:1, one launch (start us, length us, event | category | flops | bytes accessed | tf_op | source)
XLA Modules:
  0.0 81.9 jit_solution(7059354230063342250)
XLA Ops:
  0.0 79.3 %shard_map.82 = f32[2880,128]{1,0:T(8,128)} custom-call(bf16[9600,128]{1,0:T(8,128)(2,1)} %bitcast.10, f32[2880,128]{1,0:T(8,128)} %bitcast.11, f32[2880,128]{1,0:T(8,128)} %bitcast.12, bf16[300,360]{1,0:T(8,128)(2,1)} %bitcast.13, f32[300]{0:T(512)} %refs_4_.1, s32[1,32]{1,0:T(1,128)} %bitcast.14, s32[1,32]{1,0:T(1,128)} %bitcast.15, s32[32,128]{1,0:T(8,128)} %refs_7_.1), custom_call_target="tpu_custom_call" | custom-call | tf_op jit(solution)/shard_map/pallas_call | solution.py:680
  79.4 2.6 %copy.10 = f32[4,90,8,128]{3,2,1,0:T(8,128)} copy(f32[4,90,8,128]{3,2,1,0:T(8,128)} %bitcast.9) | data formatting | bytes 2949120

commit v9 on v8

--- a/solution.py
+++ b/solution.py
@@ -14,7 +14,7 @@
 EDGE = 8
 TAIL = 4
 COUNT_BASE = 64
-TILE = 256
+TILE = 512
 MESH = pl.DeviceIdType.MESH
 F32 = jnp.float32
 BF16 = jnp.bfloat16

time: 83 us -> 83 us (level)
  no operation moved by 1% of the time
where the time goes in v9:
time: 83 us; the launch traced here: 81.6 us
  Pallas kernels  79 us (95%)
  local copies, waits for them, and re-layouts  2.58 us (3%)
    pallas_call x1, Pallas kernels, per_device(): pl.pallas_call(functools.partial(main_kernel, n_lat, n_lon, planes, parts...  79 us
    unnamed x1, local copies, waits for them, and re-layouts  2.58 us

profile of v9, /device:TPU:1, one launch (start us, length us, event | category | flops | bytes accessed | tf_op | source)
XLA Modules:
  0.0 81.6 jit_solution(2416900723183201077)
XLA Ops:
  0.0 79.0 %shard_map.82 = f32[2880,128]{1,0:T(8,128)} custom-call(bf16[9600,128]{1,0:T(8,128)(2,1)} %bitcast.10, f32[2880,128]{1,0:T(8,128)} %bitcast.11, f32[2880,128]{1,0:T(8,128)} %bitcast.12, bf16[300,360]{1,0:T(8,128)(2,1)} %bitcast.13, f32[300]{0:T(512)} %refs_4_.1, s32[1,32]{1,0:T(1,128)} %bitcast.14, s32[1,32]{1,0:T(1,128)} %bitcast.15, s32[32,128]{1,0:T(8,128)} %refs_7_.1), custom_call_target="tpu_custom_call" | custom-call | tf_op jit(solution)/shard_map/pallas_call | solution.py:680
  79.0 2.6 %copy.10 = f32[4,90,8,128]{3,2,1,0:T(8,128)} copy(f32[4,90,8,128]{3,2,1,0:T(8,128)} %bitcast.9) | data formatting | bytes 2949120

commit v10 on v9

--- a/solution.py
+++ b/solution.py
@@ -611,7 +611,7 @@
         for s in range(2):
             only(2 * s - 1, lambda: row_copy(h, s).wait_recv())
 
-    @pl.loop(0, STEPS)
+    @pl.loop(0, STEPS, unroll=STEPS)
     def _(r):
         at = pl.ds(pl.multiple_of(r * width, width), width)
         put_row(total_north[:, at], r)

time: 83 us -> 82.4 us (level)
  no operation moved by 1% of the time
where the time goes in v10:
time: 82.4 us; the launch traced here: 81 us
  Pallas kernels  78.4 us (95%)
  local copies, waits for them, and re-layouts  2.58 us (3%)
    pallas_call x1, Pallas kernels, per_device(): pl.pallas_call(functools.partial(main_kernel, n_lat, n_lon, planes, parts...  78.4 us
    unnamed x1, local copies, waits for them, and re-layouts  2.58 us

profile of v10, /device:TPU:1, one launch (start us, length us, event | category | flops | bytes accessed | tf_op | source)
XLA Modules:
  0.0 81.0 jit_solution(7051894217457140228)
XLA Ops:
  0.0 78.4 %shard_map.82 = f32[2880,128]{1,0:T(8,128)} custom-call(bf16[9600,128]{1,0:T(8,128)(2,1)} %bitcast.10, f32[2880,128]{1,0:T(8,128)} %bitcast.11, f32[2880,128]{1,0:T(8,128)} %bitcast.12, bf16[300,360]{1,0:T(8,128)(2,1)} %bitcast.13, f32[300]{0:T(512)} %refs_4_.1, s32[1,32]{1,0:T(1,128)} %bitcast.14, s32[1,32]{1,0:T(1,128)} %bitcast.15, s32[32,128]{1,0:T(8,128)} %refs_7_.1), custom_call_target="tpu_custom_call" | custom-call | tf_op jit(solution)/shard_map/pallas_call | solution.py:680
  78.4 2.6 %copy.10 = f32[4,90,8,128]{3,2,1,0:T(8,128)} copy(f32[4,90,8,128]{3,2,1,0:T(8,128)} %bitcast.9) | data formatting | bytes 2949120
